TPU v7x, 128 devices: a whole 4x4x4 slice. The times are simulated.
128 devices in a mesh: col: 16 (over x, z), row: 8 (over y, core).
Axes of the slice: x: 4, y: 4, z: 4, core: 2. Of those that a mesh axis runs over, the one named last changes fastest.
Arguments:
- tokens: bfloat16 [16384, 2048], P(('col', 'row')), may hold values from -6 to 6
- route_weight: float32 [16384, 4], P(('col', 'row')), may hold values from 0.1 to 1
- expert_ids: int32 [16384, 4], P(('col', 'row')), may hold values from 0 to 127, all different within a row; in each aligned block of 128 rows (0 to 127, 128 to 255, ...) at most 8 rows name the same one
- placement: int32 [128], replicated, may hold values from 0 to 127, each once
- w_gate: bfloat16 [128, 2048, 768], P(('col', 'row')), may hold values from -0.125 to 0.125
- w_up: bfloat16 [128, 2048, 768], P(('col', 'row')), may hold values from -0.125 to 0.125
- w_down: bfloat16 [128, 768, 2048], P(('col', 'row')), may hold values from -0.21875 to 0.21875
- cotangent: bfloat16 [16384, 2048], P(('col', 'row')), may hold values from -0.59765625 to 0.59765625
Outputs:
- mixed: bfloat16 [16384, 2048], P(('col', 'row'))
- grad_tokens: bfloat16 [16384, 2048], P(('col', 'row'))
- grad_route: float32 [16384, 4], P(('col', 'row'))
- grad_gate: bfloat16 [128, 2048, 768], P(('col', 'row'))
- grad_up: bfloat16 [128, 2048, 768], P(('col', 'row'))
- grad_down: bfloat16 [128, 768, 2048], P(('col', 'row'))
Inputs may be any that keep to these rules, and one draw needn't show every extreme that they name: `expert_ids`: in each aligned block of 128 rows (the tokens of one device) every expert is named at most 8 times, a bound that some block reaches. `placement`: each expert slot serves exactly one expert.
All inputs are finite; a program needn't handle non-finite values.
Results may differ from a plain program's by a relative error of at most 0.0064.
Values may be sent and summed in bfloat16 or wider, within the bound.
No kernel may reach another device: no remote copies, remote signals or barrier semaphores. Data moves between devices by JAX's collectives and lax.ppermute only.
A program may use at most 128 MiB of HBM per device.

v0:
```python
import jax
import jax.numpy as jnp
from jax import lax
from jax.sharding import PartitionSpec as P


def expert_forward(inputs, weight_gate, weight_up, weight_down):
    gate_pre = jnp.dot(inputs, weight_gate, preferred_element_type=jnp.float32)
    up_proj = jnp.dot(inputs, weight_up, preferred_element_type=jnp.float32)
    hidden = (gate_pre * jax.nn.sigmoid(gate_pre) * up_proj).astype(jnp.bfloat16)
    outcome = jnp.dot(hidden, weight_down, preferred_element_type=jnp.float32).astype(jnp.bfloat16)
    return (outcome, gate_pre, up_proj, hidden)


def expert_backward(
    inputs, scaled_cot, gate_pre, up_proj, hidden, weight_gate, weight_up, weight_down
):
    last_last = (((1,), (1,)), ((), ()))
    d_hidden = lax.dot_general(
        scaled_cot, weight_down, last_last, preferred_element_type=jnp.float32
    )
    sigmoid_val = jax.nn.sigmoid(gate_pre)
    d_gate = (d_hidden * up_proj * sigmoid_val * (1.0 + gate_pre * (1.0 - sigmoid_val))).astype(
        jnp.bfloat16
    )
    d_up = (d_hidden * gate_pre * sigmoid_val).astype(jnp.bfloat16)
    d_inputs = (
        lax.dot_general(d_gate, weight_gate, last_last, preferred_element_type=jnp.float32)
        + lax.dot_general(d_up, weight_up, last_last, preferred_element_type=jnp.float32)
    ).astype(jnp.bfloat16)
    contract = (((0,), (0,)), ((), ()))
    grad_gate = lax.dot_general(
        inputs, d_gate, contract, preferred_element_type=jnp.float32
    ).astype(jnp.bfloat16)
    grad_up = lax.dot_general(inputs, d_up, contract, preferred_element_type=jnp.float32).astype(
        jnp.bfloat16
    )
    grad_down = lax.dot_general(
        hidden, scaled_cot, contract, preferred_element_type=jnp.float32
    ).astype(jnp.bfloat16)
    return (d_inputs, grad_gate, grad_up, grad_down)


def per_device(tokens, route_weight, expert_ids, placement, w_gate, w_up, w_down, cotangent):
    tok_dev, feature_dim = tokens.shape
    fan_out = expert_ids.shape[1]
    experts = placement.shape[0]
    slot_cap = max(2, min(tok_dev // 2, 8 * max(1, tok_dev * fan_out // (8 * experts))))
    slot_total = experts * slot_cap
    route_total = tok_dev * fan_out
    weight_gate = w_gate[0]
    weight_up = w_up[0]
    weight_down = w_down[0]
    expert_grid = jnp.arange(experts, dtype=jnp.int32)
    target = jnp.sum(jnp.where(expert_ids[..., None] == expert_grid, placement, 0), -1)
    target = target.reshape(route_total)
    one_hot = (target[:, None] == expert_grid).astype(jnp.int32)
    position = jnp.sum((jnp.cumsum(one_hot, 0) - one_hot) * one_hot, 1)
    slot_of_route = target * slot_cap + position
    scaled = (route_weight[..., None] * cotangent[:, None, :].astype(jnp.float32)).astype(
        jnp.bfloat16
    )
    scaled = scaled.reshape(route_total, feature_dim)
    selector = (jnp.arange(slot_total, dtype=jnp.int32)[:, None] == slot_of_route[None, :]).astype(
        jnp.bfloat16
    )
    token_selector = jnp.sum(selector.reshape(slot_total, tok_dev, fan_out), -1)

    def unpack_rows(buffer):
        return lax.dot_general(
            selector, buffer, (((0,), (0,)), ((), ())), preferred_element_type=jnp.float32
        )

    def dispatch(buffer, kernel):

        def itemwise(received):
            count = received.shape[1]
            outputs = kernel(received.reshape(experts * count, feature_dim))
            return tuple(
                (portion.reshape(experts, count, portion.shape[-1]) for portion in outputs)
            )

        results = itemwise(
            lax.all_to_all(
                buffer.reshape(experts, slot_cap, feature_dim),
                ("col", "row"),
                split_axis=0,
                concat_axis=0,
                tiled=True,
            )
        )
        return tuple((portion.reshape(slot_total, portion.shape[-1]) for portion in results))

    def send_back(buffer):
        returned = lax.all_to_all(
            buffer.reshape(experts, slot_cap, feature_dim),
            ("col", "row"),
            split_axis=0,
            concat_axis=0,
            tiled=True,
        )
        return returned.reshape(slot_total, feature_dim)

    def forward_kernel(inputs):
        outcome, gate_pre, up_proj, hidden = expert_forward(
            inputs, weight_gate, weight_up, weight_down
        )
        return (outcome, gate_pre, up_proj, hidden, inputs)

    def carry_kernel(inputs):
        return (inputs,)

    outcome, gate_pre, up_proj, hidden, received_tokens = dispatch(
        jnp.dot(token_selector, tokens, preferred_element_type=jnp.float32).astype(jnp.bfloat16),
        forward_kernel,
    )
    (received_scaled,) = dispatch(
        jnp.dot(selector, scaled, preferred_element_type=jnp.float32).astype(jnp.bfloat16),
        carry_kernel,
    )
    out_route = unpack_rows(send_back(outcome)).reshape(tok_dev, fan_out, feature_dim)
    mixed = jnp.sum(route_weight[..., None] * out_route, 1).astype(jnp.bfloat16)
    grad_route = jnp.sum(cotangent.astype(jnp.float32)[:, None, :] * out_route, -1)
    d_inputs, grad_gate, grad_up, grad_down = expert_backward(
        received_tokens,
        received_scaled,
        gate_pre,
        up_proj,
        hidden,
        weight_gate,
        weight_up,
        weight_down,
    )
    back_route = unpack_rows(send_back(d_inputs)).reshape(tok_dev, fan_out, feature_dim)
    grad_tokens = jnp.sum(back_route, 1).astype(jnp.bfloat16)
    return (mixed, grad_tokens, grad_route, grad_gate[None], grad_up[None], grad_down[None])


def solution(mesh):
    return jax.shard_map(
        per_device,
        mesh=mesh,
        in_specs=(
            P(("col", "row"), None),
            P(("col", "row"), None),
            P(("col", "row"), None),
            P(),
            P(("col", "row"), None, None),
            P(("col", "row"), None, None),
            P(("col", "row"), None, None),
            P(("col", "row"), None),
        ),
        out_specs=(
            P(("col", "row"), None),
            P(("col", "row"), None),
            P(("col", "row"), None),
            P(("col", "row"), None, None),
            P(("col", "row"), None, None),
            P(("col", "row"), None, None),
        ),
        check_vma=False,
    )
```

profile of v0, /device:TPU:1, one launch (start us, length us, event | category | flops | bytes accessed | tf_op | source)
XLA Modules:
  0.0 283.3 jit_solution(16135072568896893434)
XLA Ops:
  0.6 1.1 select_reduce_fusion
  1.7 0.1 copy.22
  2.1 0.1 copy.24
  2.2 0.2 fusion.53
  2.5 0.2 fusion.52
  2.9 0.3 fusion.49
  3.2 4.3 %convert_bitcast_fusion.2 = bf16[128,8,2048]{2,1,0:T(8,128)(2,1)} fusion(bf16[1024,128]{1,0:T(8,128)(2,1)S(1)} %fusion.49, bf16[128,2048]{1,0:T(8,128)(2,1)} %param.8), kind=kOutput, calls=%fused_computation.23 | convolution fusion | flops 538968064 | bytes 4980736 | tf_op jit(solution)/shard_map/dot_general | solution.py:114
  7.5 12.0 %all-to-all-start = ((bf16[128,8,2048]{2,1,0:T(8,128)(2,1)}), bf16[128,8,2048]{2,1,0:T(8,128)(2,1)}, u32[]{:S(2)}, u32[]{:S(2)}) async-start(bf16[128,8,2048]{2,1,0:T(8,128)(2,1)} %convert_bitcast_fusion.2), calls=%async_computation | async-start | bytes 8388608 | tf_op jit(solution)/shard_map/all_to_all | solution.py:84
  19.7 4.2 %mul.85.clone = f32[128,4,2048]{2,1,0:T(4,128)} broadcast(bf16[128,2048]{1,0:T(8,128)(2,1)} %param.15), dimensions={0,2} | broadcast | bytes 4718592 | tf_op jit(solution)/shard_map/mul | solution.py:60
  23.8 5.3 %mul.86 = f32[512,2048]{1,0:T(8,128)} reshape(f32[128,4,2048]{2,1,0:T(4,128)} %mul.85.clone) | data formatting | bytes 8388608 | tf_op jit(solution)/shard_map/mul | solution.py:60
  29.2 6.6 %convert_bitcast_fusion = bf16[128,8,2048]{2,1,0:T(8,128)(2,1)} fusion(f32[512,2048]{1,0:T(8,128)} %mul.86, f32[512]{0:T(512)S(1)} %mul.83, s32[512]{0:T(512)S(1)} %multiply_add_fusion.1), kind=kOutput, calls=%fused_computation.19 | convolution fusion | flops 2152202240 | bytes 8392704 | tf_op jit(solution)/shard_map/dot_general | solution.py:118
  35.7 36.2 %all-to-all-done = bf16[128,8,2048]{2,1,0:T(8,128)(2,1)} async-done(((bf16[128,8,2048]{2,1,0:T(8,128)(2,1)}), bf16[128,8,2048]{2,1,0:T(8,128)(2,1)}, u32[]{:S(2)}, u32[]{:S(2)}) %all-to-all-start) | async-done | bytes 4194336 | tf_op jit(solution)/shard_map/all_to_all | solution.py:84
  72.0 16.9 %all-to-all-start.2 = ((bf16[128,8,2048]{2,1,0:T(8,128)(2,1)}), bf16[128,8,2048]{2,1,0:T(8,128)(2,1)}, u32[]{:S(2)}, u32[]{:S(2)}) async-start(bf16[128,8,2048]{2,1,0:T(8,128)(2,1)} %convert_bitcast_fusion), calls=%async_computation.2 | async-start | bytes 8388608 | tf_op jit(solution)/shard_map/all_to_all | solution.py:84
  88.9 8.4 %fusion.13 = f32[1024,768]{1,0:T(8,128)} fusion(bf16[128,8,2048]{2,1,0:T(8,128)(2,1)} %all-to-all-done, bf16[1,2048,768]{2,1,0:T(8,128)(2,1)} %param.13), kind=kOutput, calls=%fused_computation.14 | convolution fusion | flops 3221225472 | bytes 10485760 | tf_op jit(solution)/shard_map/dot_general | solution.py:9
  97.3 7.3 %fusion.15 = f32[1024,768]{1,0:T(8,128)} fusion(bf16[128,8,2048]{2,1,0:T(8,128)(2,1)} %all-to-all-done, bf16[1,2048,768]{2,1,0:T(8,128)(2,1)S(1)} %copy-done.3), kind=kOutput, calls=%fused_computation.16 | convolution fusion | flops 3221225472 | bytes 10485760 | tf_op jit(solution)/shard_map/dot_general | solution.py:8
  104.6 36.7 %all-to-all-done.2 = bf16[128,8,2048]{2,1,0:T(8,128)(2,1)} async-done(((bf16[128,8,2048]{2,1,0:T(8,128)(2,1)}), bf16[128,8,2048]{2,1,0:T(8,128)(2,1)}, u32[]{:S(2)}, u32[]{:S(2)}) %all-to-all-start.2) | async-done | bytes 4194336 | tf_op jit(solution)/shard_map/all_to_all | solution.py:84
  141.3 9.7 %multiply_convert_fusion.1 = (bf16[1024,768]{1,0:T(8,128)(2,1)S(1)}, bf16[1024,768]{1,0:T(8,128)(2,1)S(1)}, bf16[1024,768]{1,0:T(8,128)(2,1)}) fusion(f32[1024,768]{1,0:T(8,128)} %fusion.15, f32[1024,768]{1,0:T(8,128)} %fusion.13, bf16[1,768,2048]{2,1,0:T(8,128)(2,1)S(1)} %copy-done, bf16[128,8,2048]{2,1,0:T(8,128)(2,1)} %all-to-all-done.2), kind=kOutput, calls=%fused_computation.34 | convolution fusion | flops 3233808384 | bytes 18350080 | tf_op jit(solution)/shard_map/dot_general | solution.py:19
  151.0 3.4 %fusion.30 = f32[1024,2048]{1,0:T(8,128)S(1)} fusion(bf16[1024,768]{1,0:T(8,128)(2,1)S(1)} %get-tuple-element.9, bf16[1,2048,768]{2,1,0:T(8,128)(2,1)S(1)} %copy-done.4), kind=kOutput, calls=%fused_computation.31 | convolution fusion | flops 3221225472 | bytes 13107200 | tf_op jit(solution)/shard_map/dot_general | solution.py:28
  154.5 5.0 %fusion = bf16[128,8,2048]{2,1,0:T(8,128)(2,1)} fusion(f32[1024,2048]{1,0:T(8,128)S(1)} %fusion.30, bf16[1024,768]{1,0:T(8,128)(2,1)S(1)} %get-tuple-element.8, bf16[1,2048,768]{2,1,0:T(8,128)(2,1)S(1)} %copy-done.5), kind=kOutput, calls=%fused_computation.1 | convolution fusion | flops 3225419776 | bytes 17301504 | tf_op jit(solution)/shard_map/dot_general | solution.py:29
  159.6 6.0 %all-to-all-start.3 = ((bf16[128,8,2048]{2,1,0:T(8,128)(2,1)}), bf16[128,8,2048]{2,1,0:T(8,128)(2,1)}, u32[]{:S(2)}, u32[]{:S(2)}) async-start(bf16[128,8,2048]{2,1,0:T(8,128)(2,1)} %fusion), calls=%async_computation.3 | async-start | bytes 8388608 | tf_op jit(solution)/shard_map/all_to_all | solution.py:95
  165.5 6.4 %convert_bitcast_fusion.1 = bf16[128,8,2048]{2,1,0:T(8,128)(2,1)} fusion(bf16[1024,768]{1,0:T(8,128)(2,1)} %get-tuple-element.10, bf16[1,768,2048]{2,1,0:T(8,128)(2,1)S(1)} %copy-done), kind=kOutput, calls=%fused_computation.22 | convolution fusion | flops 3223322624 | bytes 8912896 | tf_op jit(solution)/shard_map/dot_general | solution.py:11
  171.9 46.2 %all-to-all-done.3 = bf16[128,8,2048]{2,1,0:T(8,128)(2,1)} async-done(((bf16[128,8,2048]{2,1,0:T(8,128)(2,1)}), bf16[128,8,2048]{2,1,0:T(8,128)(2,1)}, u32[]{:S(2)}, u32[]{:S(2)}) %all-to-all-start.3) | async-done | bytes 4194336 | tf_op jit(solution)/shard_map/all_to_all | solution.py:95
  218.1 6.1 %all-to-all-start.1 = ((bf16[128,8,2048]{2,1,0:T(8,128)(2,1)}), bf16[128,8,2048]{2,1,0:T(8,128)(2,1)}, u32[]{:S(2)}, u32[]{:S(2)}) async-start(bf16[128,8,2048]{2,1,0:T(8,128)(2,1)} %convert_bitcast_fusion.1), calls=%async_computation.1 | async-start | bytes 8388608 | tf_op jit(solution)/shard_map/all_to_all | solution.py:95
  224.1 2.1 convert_element_type.65
  226.3 1.2 iota_compare_fusion.2
  227.4 2.1 eq.87
  229.5 7.9 %fusion.33 = bf16[1,768,2048]{2,1,0:T(8,128)(2,1)} fusion(bf16[1024,768]{1,0:T(8,128)(2,1)} %get-tuple-element.10, bf16[128,8,2048]{2,1,0:T(8,128)(2,1)} %all-to-all-done.2), kind=kOutput, calls=%fused_computation.38 | convolution fusion | flops 3222798336 | bytes 8912896 | tf_op jit(solution)/shard_map/dot_general | solution.py:38
  237.5 7.5 %fusion.36 = bf16[1,2048,768]{2,1,0:T(8,128)(2,1)} fusion(bf16[1024,768]{1,0:T(8,128)(2,1)S(1)} %copy-done.9, bf16[128,8,2048]{2,1,0:T(8,128)(2,1)} %all-to-all-done), kind=kOutput, calls=%fused_computation.39 | convolution fusion | flops 3222798336 | bytes 8912896 | tf_op jit(solution)/shard_map/dot_general | solution.py:35
  245.0 7.4 %fusion.39 = bf16[1,2048,768]{2,1,0:T(8,128)(2,1)} fusion(bf16[1024,768]{1,0:T(8,128)(2,1)S(1)} %copy-done.7, bf16[128,8,2048]{2,1,0:T(8,128)(2,1)} %all-to-all-done), kind=kOutput, calls=%fused_computation.40 | convolution fusion | flops 3222798336 | bytes 8912896 | tf_op jit(solution)/shard_map/dot_general | solution.py:32
  252.4 5.6 %fusion.44 = bf16[128,2048]{1,0:T(8,128)(2,1)} fusion(bf16[128,8,2048]{2,1,0:T(8,128)(2,1)} %all-to-all-done.3, pred[128,4,1024]{2,1,0:T(4,128)(4,1)S(1)} %copy-done.1), kind=kOutput, calls=%fused_computation.46 | convolution fusion | flops 2148270080 | bytes 5242880 | tf_op jit(solution)/shard_map/dot_general | solution.py:70
  258.1 18.6 %all-to-all-done.1 = bf16[128,8,2048]{2,1,0:T(8,128)(2,1)} async-done(((bf16[128,8,2048]{2,1,0:T(8,128)(2,1)}), bf16[128,8,2048]{2,1,0:T(8,128)(2,1)}, u32[]{:S(2)}, u32[]{:S(2)}) %all-to-all-start.1) | async-done | bytes 4194336 | tf_op jit(solution)/shard_map/all_to_all | solution.py:95
  276.7 6.2 %multiply_reduce_fusion = (f32[128,4]{0,1:T(4,128)}, bf16[128,2048]{1,0:T(8,128)(2,1)}) fusion(f32[128,2048]{1,0:T(8,128)} %convert_element_type.65, f32[128,4]{0,1:T(4,128)S(1)} %copy-done.2, bf16[128,8,2048]{2,1,0:T(8,128)(2,1)} %all-to-all-done.1, pred[128,4,1024]{2,1,0:T(4,128)(4,1)} %eq.87), kind=kOutput, calls=%fused_computation.18 | convolution fusion | flops 2151415296 | bytes 6295552 | tf_op jit(solution)/shard_map/dot_general | solution.py:70
  (34 shorter events, 0.7 us)
Async XLA Ops:
  0.6 140.6 %copy-start = (bf16[1,768,2048]{2,1,0:T(8,128)(2,1)S(1)}, bf16[1,768,2048]{2,1,0:T(8,128)(2,1)}, u32[]{:S(2)}) copy-start(bf16[1,768,2048]{2,1,0:T(8,128)(2,1)} %param.14) | copy-start | bytes 9437188
  7.5 12.0 %copy-start.2 = (f32[128,4]{0,1:T(4,128)S(1)}, f32[128,4]{0,1:T(4,128)}, u32[]{:S(2)}) copy-start(f32[128,4]{0,1:T(4,128)} %param.9) | copy-start | bytes 6148
  7.5 64.5 %all-to-all-start = ((bf16[128,8,2048]{2,1,0:T(8,128)(2,1)}), bf16[128,8,2048]{2,1,0:T(8,128)(2,1)}, u32[]{:S(2)}, u32[]{:S(2)}) async-start(bf16[128,8,2048]{2,1,0:T(8,128)(2,1)} %convert_bitcast_fusion.2), calls=%async_computation | async-start | bytes 8388608 | tf_op jit(solution)/shard_map/all_to_all | solution.py:84
  72.0 69.3 %all-to-all-start.2 = ((bf16[128,8,2048]{2,1,0:T(8,128)(2,1)}), bf16[128,8,2048]{2,1,0:T(8,128)(2,1)}, u32[]{:S(2)}, u32[]{:S(2)}) async-start(bf16[128,8,2048]{2,1,0:T(8,128)(2,1)} %convert_bitcast_fusion), calls=%async_computation.2 | async-start | bytes 8388608 | tf_op jit(solution)/shard_map/all_to_all | solution.py:84
  88.9 8.4 %copy-start.3 = (bf16[1,2048,768]{2,1,0:T(8,128)(2,1)S(1)}, bf16[1,2048,768]{2,1,0:T(8,128)(2,1)}, u32[]{:S(2)}) copy-start(bf16[1,2048,768]{2,1,0:T(8,128)(2,1)} %param.12) | copy-start | bytes 9437188
  141.3 9.8 %copy-start.4 = (bf16[1,2048,768]{2,1,0:T(8,128)(2,1)S(1)}, bf16[1,2048,768]{2,1,0:T(8,128)(2,1)}, u32[]{:S(2)}) copy-start(bf16[1,2048,768]{2,1,0:T(8,128)(2,1)} %param.12) | copy-start | bytes 9437188
  151.0 3.5 %copy-start.6 = (bf16[1024,768]{1,0:T(8,128)(2,1)}, bf16[1024,768]{1,0:T(8,128)(2,1)S(1)}, u32[]{:S(2)}) copy-start(bf16[1024,768]{1,0:T(8,128)(2,1)S(1)} %get-tuple-element.9) | copy-start | bytes 4718596
  151.0 3.5 %copy-start.8 = (bf16[1024,768]{1,0:T(8,128)(2,1)}, bf16[1024,768]{1,0:T(8,128)(2,1)S(1)}, u32[]{:S(2)}) copy-start(bf16[1024,768]{1,0:T(8,128)(2,1)S(1)} %get-tuple-element.8) | copy-start | bytes 4718596
  151.0 3.5 %copy-start.5 = (bf16[1,2048,768]{2,1,0:T(8,128)(2,1)S(1)}, bf16[1,2048,768]{2,1,0:T(8,128)(2,1)}, u32[]{:S(2)}) copy-start(bf16[1,2048,768]{2,1,0:T(8,128)(2,1)} %param.13) | copy-start | bytes 9437188
  159.6 58.5 %all-to-all-start.3 = ((bf16[128,8,2048]{2,1,0:T(8,128)(2,1)}), bf16[128,8,2048]{2,1,0:T(8,128)(2,1)}, u32[]{:S(2)}, u32[]{:S(2)}) async-start(bf16[128,8,2048]{2,1,0:T(8,128)(2,1)} %fusion), calls=%async_computation.3 | async-start | bytes 8388608 | tf_op jit(solution)/shard_map/all_to_all | solution.py:95
  218.1 58.6 %all-to-all-start.1 = ((bf16[128,8,2048]{2,1,0:T(8,128)(2,1)}), bf16[128,8,2048]{2,1,0:T(8,128)(2,1)}, u32[]{:S(2)}, u32[]{:S(2)}) async-start(bf16[128,8,2048]{2,1,0:T(8,128)(2,1)} %convert_bitcast_fusion.1), calls=%async_computation.1 | async-start | bytes 8388608 | tf_op jit(solution)/shard_map/all_to_all | solution.py:95
  229.5 7.9 %copy-start.9 = (bf16[1024,768]{1,0:T(8,128)(2,1)S(1)}, bf16[1024,768]{1,0:T(8,128)(2,1)}, u32[]{:S(2)}) copy-start(bf16[1024,768]{1,0:T(8,128)(2,1)} %copy-done.8) | copy-start | bytes 4718596
  237.5 7.5 %copy-start.7 = (bf16[1024,768]{1,0:T(8,128)(2,1)S(1)}, bf16[1024,768]{1,0:T(8,128)(2,1)}, u32[]{:S(2)}) copy-start(bf16[1024,768]{1,0:T(8,128)(2,1)} %copy-done.6) | copy-start | bytes 4718596
  245.0 7.5 %copy-start.1 = (pred[128,4,1024]{2,1,0:T(4,128)(4,1)S(1)}, pred[128,4,1024]{2,1,0:T(4,128)(4,1)}, u32[]{:S(2)}) copy-start(pred[128,4,1024]{2,1,0:T(4,128)(4,1)} %eq.87) | copy-start | bytes 1572868
where the time goes:
time: 284 us; the launch traced here: 283 us
  waiting for transfers between devices  138 us (49%)
  matrix products  85.8 us (30%)
  starting transfers between devices  40.9 us (14%)
  local copies, waits for them, and re-layouts  12.5 us (4%)
  other arithmetic  5.14 us (2%)
    all_to_all x2, waiting for transfers between devices, dispatch(): lax.all_to_all(buffer.reshape(experts, slot_cap, feature_dim), ('col', 'r...  72.9 us
    all_to_all x2, waiting for transfers between devices, send_back(): lax.all_to_all(buffer.reshape(experts, slot_cap, feature_dim), ('col', 'r...  64.7 us
    all_to_all x2, starting transfers between devices, dispatch(): lax.all_to_all(buffer.reshape(experts, slot_cap, feature_dim), ('col', 'r...  28.9 us
    all_to_all x2, starting transfers between devices, send_back(): lax.all_to_all(buffer.reshape(experts, slot_cap, feature_dim), ('col', 'r...  12 us
    dot_general x2, matrix products, unpack_rows(): lax.dot_general(selector, buffer, (((0,), (0,)), ((), ())), preferred_ele...  11.8 us
    dot_general x1, matrix products, expert_backward(): lax.dot_general(scaled_cot, weight_down, last_last, preferred_element_typ...  9.75 us
    mul x2, local copies, waits for them, and re-layouts, per_device(): route_weight[..., None] * cotangent[:, None, :].astype(jnp.float32)  9.49 us
    dot_general x1, matrix products, expert_forward(): up_proj = jnp.dot(inputs, weight_up, preferred_element_type=jnp.float32)  8.37 us
  transfers between devices with their start and end apart: 4, of which 4 were waited for; matrix products, arithmetic and copies ran while one was open for 26% of the time, Pallas kernels for 0%

commit v1 on v0

v1 whole, which is shorter than its diff:
```python
import functools
import jax
import jax.numpy as jnp
from jax import lax
from jax.experimental import pallas as pl
from jax.experimental.pallas import tpu as pltpu
from jax.sharding import PartitionSpec as P

BF16 = jnp.bfloat16
F32 = jnp.float32
LAST_LAST = (((1,), (1,)), ((), ()))
FIRST_FIRST = (((0,), (0,)), ((), ()))
VMEM_LIMIT = 56 * 1024 * 1024


def iota(shape, dim):
    return lax.broadcasted_iota(jnp.int32, shape, dim)


def dot(a, b, dims=(((1,), (0,)), ((), ()))):
    return lax.dot_general(a, b, dims, preferred_element_type=F32)


def route_slots(ids, placement, cap):
    top, tokens = ids.shape
    experts = placement.shape[1]
    expert = iota((experts, tokens), 0)
    hits = [ids[k : k + 1, :] == expert for k in range(top)]
    named = functools.reduce(jnp.logical_or, hits)
    earlier = (iota((tokens, tokens), 0) < iota((tokens, tokens), 1)).astype(F32)
    count = dot(named.astype(F32).astype(BF16), earlier.astype(BF16)).astype(jnp.int32)
    diagonal = iota((experts, experts), 0) == iota((experts, experts), 1)
    serving = jnp.sum(jnp.where(diagonal, placement, 0), 1, keepdims=True)
    slot = serving * cap + count
    return jnp.concatenate(
        [jnp.sum(jnp.where(hit, slot, 0), 0, keepdims=True) for hit in hits], 0
    )


def selectors(slots, weights, first, rows):
    top, tokens = slots.shape
    row = iota((rows, tokens), 0) + first
    hits = [row == slots[k : k + 1, :] for k in range(top)]
    chosen = functools.reduce(jnp.logical_or, hits)
    weight = functools.reduce(
        jnp.add, [jnp.where(hits[k], weights[k : k + 1, :], 0.0) for k in range(top)]
    )
    high = weight.astype(BF16)
    low = (weight - high.astype(F32)).astype(BF16)
    return hits, chosen.astype(F32).astype(BF16), high, low


def pack_kernel(cap, ids_ref, placement_ref, weight_ref, tokens_ref, cot_ref, out_ref, slots_ref):
    rows = out_ref.shape[0]
    width = tokens_ref.shape[1]

    @pl.when(pl.program_id(0) == 0)
    def _():
        slots_ref[...] = route_slots(ids_ref[...], placement_ref[...], cap)

    _, chosen, high, low = selectors(
        slots_ref[...], weight_ref[...], pl.program_id(0) * rows, rows
    )
    out_ref[:, :width] = dot(chosen, tokens_ref[...]).astype(BF16)
    cot = cot_ref[...]
    out_ref[:, width:] = (dot(high, cot) + dot(low, cot)).astype(BF16)


def pack(ids, placement, weights, tokens, cotangent, cap):
    top, tok_dev = ids.shape
    experts = placement.shape[1]
    width = tokens.shape[1]
    total = experts * cap
    block = min(total, 256)
    whole = lambda shape: pl.BlockSpec(shape, lambda i: (0, 0))
    return pl.pallas_call(
        functools.partial(pack_kernel, cap),
        grid=(total // block,),
        in_specs=[
            whole((top, tok_dev)),
            whole((1, experts)),
            whole((top, tok_dev)),
            whole((tok_dev, width)),
            whole((tok_dev, width)),
        ],
        out_specs=[
            pl.BlockSpec((block, 2 * width), lambda i: (i, 0)),
            whole((top, tok_dev)),
        ],
        out_shape=[
            jax.ShapeDtypeStruct((total, 2 * width), BF16),
            jax.ShapeDtypeStruct((top, tok_dev), jnp.int32),
        ],
        compiler_params=pltpu.CompilerParams(vmem_limit_bytes=VMEM_LIMIT),
        name="pack",
    )(ids, placement, weights, tokens, cotangent)


def expert_kernel(rows_ref, gate_ref, up_ref, down_ref, back_ref, hidden_ref, dgate_ref, dup_ref):
    width = gate_ref.shape[0]
    inputs = rows_ref[:, :width]
    gate_pre = dot(inputs, gate_ref[...])
    up_proj = dot(inputs, up_ref[...])
    sig = jax.nn.sigmoid(gate_pre)
    silu = gate_pre * sig
    hidden = (silu * up_proj).astype(BF16)
    hidden_ref[...] = hidden
    back_ref[:, :width] = dot(hidden, down_ref[...]).astype(BF16)
    d_hidden = dot(rows_ref[:, width:], down_ref[...], LAST_LAST)
    d_gate = (d_hidden * up_proj * sig * (1.0 + gate_pre * (1.0 - sig))).astype(BF16)
    d_up = (d_hidden * silu).astype(BF16)
    dgate_ref[...] = d_gate
    dup_ref[...] = d_up
    back_ref[:, width:] = (
        dot(d_gate, gate_ref[...], LAST_LAST) + dot(d_up, up_ref[...], LAST_LAST)
    ).astype(BF16)


def expert(rows, w_gate, w_up, w_down):
    total, double = rows.shape
    width, hidden = w_gate.shape
    block = min(total, 256)
    strip = lambda n: pl.BlockSpec((block, n), lambda i: (i, 0))
    resident = pl.BlockSpec(memory_space=pltpu.VMEM)
    return pl.pallas_call(
        expert_kernel,
        grid=(total // block,),
        in_specs=[strip(double), resident, resident, resident],
        out_specs=[strip(double), strip(hidden), strip(hidden), strip(hidden)],
        out_shape=[jax.ShapeDtypeStruct((total, double), BF16)]
        + [jax.ShapeDtypeStruct((total, hidden), BF16)] * 3,
        compiler_params=pltpu.CompilerParams(vmem_limit_bytes=VMEM_LIMIT),
        cost_estimate=pl.CostEstimate(
            flops=12 * total * width * hidden, bytes_accessed=2 * total * double * 2, transcendentals=0
        ),
        name="expert",
    )(rows, w_gate, w_up, w_down)


def unpack_kernel(slots_ref, weight_ref, cot_ref, out_ref, din_ref, mixed_ref, gtok_ref, groute_ref, sel_ref, dots_ref):
    step = pl.program_id(0)
    total = out_ref.shape[0]
    tok_dev = cot_ref.shape[0]
    top = slots_ref.shape[0]

    @pl.when(step == 0)
    def _():
        _, chosen, high, low = selectors(slots_ref[...], weight_ref[...], 0, total)
        sel_ref[:, :tok_dev] = high
        sel_ref[:, tok_dev : 2 * tok_dev] = low
        sel_ref[:, 2 * tok_dev :] = chosen
        dots_ref[...] = jnp.zeros_like(dots_ref)

    outcome = out_ref[...]
    halves = dot(sel_ref[:, : 2 * tok_dev], outcome, FIRST_FIRST)
    mixed_ref[...] = (halves[:tok_dev] + halves[tok_dev:]).astype(BF16)
    gtok_ref[...] = dot(sel_ref[:, 2 * tok_dev :], din_ref[...], FIRST_FIRST).astype(BF16)
    dots_ref[...] += dot(outcome, cot_ref[...], LAST_LAST)

    @pl.when(step == pl.num_programs(0) - 1)
    def _():
        slots = slots_ref[...]
        row = iota((total, tok_dev), 0)
        dots = dots_ref[...]
        groute_ref[...] = jnp.concatenate(
            [
                jnp.sum(jnp.where(row == slots[k : k + 1, :], dots, 0.0), 0, keepdims=True)
                for k in range(top)
            ],
            0,
        )


def unpack(slots, weights, cotangent, returned):
    top, tok_dev = slots.shape
    width = cotangent.shape[1]
    total = returned.shape[0]
    block = min(width, 512)
    steps = width // block
    whole = lambda shape: pl.BlockSpec(shape, lambda i: (0, 0))
    return pl.pallas_call(
        unpack_kernel,
        grid=(steps,),
        in_specs=[
            whole((top, tok_dev)),
            whole((top, tok_dev)),
            pl.BlockSpec((tok_dev, block), lambda i: (0, i)),
            pl.BlockSpec((total, block), lambda i: (0, i)),
            pl.BlockSpec((total, block), lambda i: (0, i + steps)),
        ],
        out_specs=[
            pl.BlockSpec((tok_dev, block), lambda i: (0, i)),
            pl.BlockSpec((tok_dev, block), lambda i: (0, i)),
            whole((top, tok_dev)),
        ],
        out_shape=[
            jax.ShapeDtypeStruct((tok_dev, width), BF16),
            jax.ShapeDtypeStruct((tok_dev, width), BF16),
            jax.ShapeDtypeStruct((top, tok_dev), F32),
        ],
        scratch_shapes=[
            pltpu.VMEM((total, 3 * tok_dev), BF16),
            pltpu.VMEM((total, tok_dev), F32),
        ],
        compiler_params=pltpu.CompilerParams(vmem_limit_bytes=VMEM_LIMIT),
        name="unpack",
    )(slots, weights, cotangent, returned, returned)


def exchange(buffer, experts):
    total, width = buffer.shape
    moved = lax.all_to_all(
        buffer.reshape(experts, total // experts, width),
        ("col", "row"),
        split_axis=0,
        concat_axis=0,
        tiled=True,
    )
    return moved.reshape(total, width)


def per_device(tokens, route_weight, expert_ids, placement, w_gate, w_up, w_down, cotangent):
    tok_dev, width = tokens.shape
    fan_out = expert_ids.shape[1]
    experts = placement.shape[0]
    cap = max(2, min(tok_dev // 2, 8 * max(1, tok_dev * fan_out // (8 * experts))))
    weights = route_weight.T
    packed, slots = pack(
        expert_ids.T, placement.reshape(1, experts), weights, tokens, cotangent, cap
    )
    received = exchange(packed, experts)
    back, hidden, d_gate, d_up = expert(received, w_gate[0], w_up[0], w_down[0])
    returned = exchange(back, experts)
    inputs = received[:, :width]
    scaled = received[:, width:]
    grad_gate = dot(inputs, d_gate, FIRST_FIRST).astype(BF16)
    grad_up = dot(inputs, d_up, FIRST_FIRST).astype(BF16)
    grad_down = dot(hidden, scaled, FIRST_FIRST).astype(BF16)
    mixed, grad_tokens, grad_route = unpack(slots, weights, cotangent, returned)
    return (mixed, grad_tokens, grad_route.T, grad_gate[None], grad_up[None], grad_down[None])


def solution(mesh):
    split = P(("col", "row"), None)
    split3 = P(("col", "row"), None, None)
    return jax.shard_map(
        per_device,
        mesh=mesh,
        in_specs=(split, split, split, P(), split3, split3, split3, split),
        out_specs=(split, split, split, split3, split3, split3),
        check_vma=False,
    )
```

time: 284 us -> 270 us (0.951)
  blocking collectives: 0 us -> 110 us
  matrix products: 85.8 us -> 17.1 us
  waiting for transfers between devices: 138 us -> 89.1 us
  Pallas kernels: 0 us -> 44.4 us
  starting transfers between devices: 40.9 us -> 8.1 us
  local copies, waits for them, and re-layouts: 12.5 us -> 0.02 us
  other arithmetic: 5.14 us -> 0 us
    all_to_all x0 -> x1, blocking collectives: none -> 110 us  [exchange(): lax.all_to_all(buffer.reshape(experts, total // experts, width), ('col',...]
    dot_general x13 -> x3, matrix products: 85.8 us -> 17.1 us  [dot(): return lax.dot_general(a, b, dims, preferred_element_type=F32)]
    all_to_all x4 -> x1, waiting for transfers between devices: 138 us -> 89.1 us  [exchange(): lax.all_to_all(buffer.reshape(experts, total // experts, width), ('col',...]
    pallas_call x0 -> x3, Pallas kernels: none -> 44.4 us  [the longest x1 29.4 us: expert(): pl.pallas_call(expert_kernel, grid=(total // block,), in_specs=[strip(dou...]
    all_to_all x4 -> x1, starting transfers between devices: 40.9 us -> 8.1 us  [exchange(): lax.all_to_all(buffer.reshape(experts, total // experts, width), ('col',...]
    mul x3 -> x0, local copies, waits for them, and re-layouts: 9.6 us -> none  [the longest x2 9.49 us: per_device(): route_weight[..., None] * cotangent[:, None, :].astype(jnp.float32)]
  transfers between devices with their start and end apart: 4 -> 1, of which waited for: 4 -> 1; matrix products, arithmetic and copies ran while one was open for 26% -> 6% of each run, Pallas kernels for 0% -> 0%
where the time goes in v1:
time: 270 us
  blocking collectives  110 us (41%)
  waiting for transfers between devices  89.1 us (33%)
  Pallas kernels  44.4 us (16%)
  matrix products  17.1 us (6%)
  starting transfers between devices  8.1 us (3%)
    all_to_all x1, blocking collectives, exchange(): lax.all_to_all(buffer.reshape(experts, total // experts, width), ('col',...  110 us
    all_to_all x1, waiting for transfers between devices, exchange(): lax.all_to_all(buffer.reshape(experts, total // experts, width), ('col',...  89.1 us
    pallas_call x1, Pallas kernels, expert(): pl.pallas_call(expert_kernel, grid=(total // block,), in_specs=[strip(dou...  29.4 us
    dot_general x3, matrix products, dot(): return lax.dot_general(a, b, dims, preferred_element_type=F32)  17.1 us
    all_to_all x1, starting transfers between devices, exchange(): lax.all_to_all(buffer.reshape(experts, total // experts, width), ('col',...  8.1 us
    pallas_call x1, Pallas kernels, unpack(): pl.pallas_call(unpack_kernel, grid=(steps,), in_specs=[whole((top, tok_de...  7.86 us
    pallas_call x1, Pallas kernels, pack(): pl.pallas_call(functools.partial(pack_kernel, cap), grid=(total // block,...  7.16 us
  transfers between devices with their start and end apart: 1, of which 1 were waited for; matrix products, arithmetic and copies ran while one was open for 6% of the time, Pallas kernels for 0%

profile of v1, /device:TPU:1, one launch (start us, length us, event | category | flops | bytes accessed | tf_op | source)
XLA Modules:
  0.0 269.6 jit_solution(4469441859426470338)
XLA Ops:
  0.6 7.2 %pack.1 = (bf16[1024,4096]{1,0:T(8,128)(2,1)}, s32[4,128]{1,0:T(4,128)}) custom-call(s32[4,128]{1,0:T(4,128)} %bitcast.28, s32[1,128]{1,0:T(1,128)} %bitcast.29, f32[4,128]{1,0:T(4,128)} %bitcast.26, bf16[128,2048]{1,0:T(8,128)(2,1)} %tokens_ref.1, bf16[128,2048]{1,0:T(8,128)(2,1)} %cot_ref.3), custom_call_target="tpu_custom_call" | custom-call | tf_op jit(solution)/shard_map/pack/pallas_call | solution.py:76
  7.8 110.0 %all_to_all.10 = bf16[128,8,4096]{2,1,0:T(8,128)(2,1)} all-to-all(bf16[128,8,4096]{2,1,0:T(8,128)(2,1)} %bitcast.25), channel_id=1, replica_groups=mesh['col'=16,'row'=8] {'col','row'}, dimensions={0} | all-to-all | bytes 16777216 | tf_op jit(solution)/shard_map/all_to_all | solution.py:212
  117.8 29.4 %expert.1 = (bf16[1024,4096]{1,0:T(8,128)(2,1)}, bf16[1024,768]{1,0:T(8,128)(2,1)}, bf16[1024,768]{1,0:T(8,128)(2,1)}, bf16[1024,768]{1,0:T(8,128)(2,1)}) custom-call(bf16[1024,4096]{1,0:T(8,128)(2,1)} %bitcast.20, bf16[2048,768]{1,0:T(8,128)(2,1)} %bitcast.30, bf16[2048,768]{1,0:T(8,128)(2,1)} %bitcast.31, bf16[768,2048]{1,0:T(8,128)(2,1)} %bitcast.32), custom_call_target="tpu_custom_call" | custom-call | flops 19327352832 | bytes 16777216 | tf_op jit(solution)/shard_map/expert/pallas_call | solution.py:125
  147.2 0.0 copy-start.1
  147.2 8.1 %all-to-all-start.1 = ((bf16[128,8,4096]{2,1,0:T(8,128)(2,1)}), bf16[128,8,4096]{2,1,0:T(8,128)(2,1)}, u32[]{:S(2)}, u32[]{:S(2)}) async-start(bf16[128,8,4096]{2,1,0:T(8,128)(2,1)} %bitcast.24), calls=%async_computation.1 | async-start | bytes 16777216 | tf_op jit(solution)/shard_map/all_to_all | solution.py:212
  155.3 0.0 copy-done.1
  155.3 0.0 copy-start
  155.4 0.0 copy-start.3
  155.4 7.2 %fusion.15 = bf16[1,768,2048]{2,1,0:T(8,128)(2,1)} fusion(bf16[1024,768]{1,0:T(8,128)(2,1)S(1)} %copy-done.1, bf16[1024,4096]{1,0:T(8,128)(2,1)} %bitcast.21), kind=kOutput, calls=%fused_computation.9 | convolution fusion | flops 3222798336 | bytes 8912896 | tf_op jit(solution)/shard_map/dot_general | solution.py:21
  162.6 0.0 copy-done
  162.6 0.0 copy-done.3
  162.6 0.0 copy-start.2
  162.6 5.0 %fusion.18 = bf16[1,2048,768]{2,1,0:T(8,128)(2,1)} fusion(bf16[1024,768]{1,0:T(8,128)(2,1)S(1)} %copy-done.3, bf16[1024,4096]{1,0:T(8,128)(2,1)S(1)} %bitcast.22), kind=kOutput, calls=%fused_computation.10 | convolution fusion | flops 3222798336 | bytes 8912896 | tf_op jit(solution)/shard_map/dot_general | solution.py:21
  167.5 0.0 copy-done.2
  167.5 4.9 %fusion.21 = bf16[1,2048,768]{2,1,0:T(8,128)(2,1)} fusion(bf16[1024,768]{1,0:T(8,128)(2,1)S(1)} %copy-done.2, bf16[1024,4096]{1,0:T(8,128)(2,1)S(1)} %bitcast.23), kind=kOutput, calls=%fused_computation.11 | convolution fusion | flops 3222798336 | bytes 8912896 | tf_op jit(solution)/shard_map/dot_general | solution.py:21
  172.5 89.1 %all-to-all-done.1 = bf16[128,8,4096]{2,1,0:T(8,128)(2,1)} async-done(((bf16[128,8,4096]{2,1,0:T(8,128)(2,1)}), bf16[128,8,4096]{2,1,0:T(8,128)(2,1)}, u32[]{:S(2)}, u32[]{:S(2)}) %all-to-all-start.1) | async-done | bytes 8388640 | tf_op jit(solution)/shard_map/all_to_all | solution.py:212
  261.6 7.9 %unpack.1 = (bf16[128,2048]{1,0:T(8,128)(2,1)}, bf16[128,2048]{1,0:T(8,128)(2,1)}, f32[4,128]{1,0:T(4,128)}) custom-call(s32[4,128]{1,0:T(4,128)} %get-tuple-element.15.slots_ref, f32[4,128]{1,0:T(4,128)} %bitcast.27, bf16[128,2048]{1,0:T(8,128)(2,1)} %cot_ref.3, bf16[1024,4096]{1,0:T(8,128)(2,1)} %bitcast.9.out_ref.din_ref, ...), custom_call_target="tpu_custom_call" | custom-call | tf_op jit(solution)/shard_map/unpack/pallas_call | solution.py:181
Async XLA Ops:
  147.2 8.1 %copy-start.1 = (bf16[1024,768]{1,0:T(8,128)(2,1)S(1)}, bf16[1024,768]{1,0:T(8,128)(2,1)}, u32[]{:S(2)}) copy-start(bf16[1024,768]{1,0:T(8,128)(2,1)} %get-tuple-element.23) | copy-start | bytes 4718596
  147.2 114.4 %all-to-all-start.1 = ((bf16[128,8,4096]{2,1,0:T(8,128)(2,1)}), bf16[128,8,4096]{2,1,0:T(8,128)(2,1)}, u32[]{:S(2)}, u32[]{:S(2)}) async-start(bf16[128,8,4096]{2,1,0:T(8,128)(2,1)} %bitcast.24), calls=%async_computation.1 | async-start | bytes 16777216 | tf_op jit(solution)/shard_map/all_to_all | solution.py:212
  155.3 7.2 %copy-start = (bf16[128,8,4096]{2,1,0:T(8,128)(2,1)S(1)}, bf16[128,8,4096]{2,1,0:T(8,128)(2,1)}, u32[]{:S(2)}) copy-start(bf16[128,8,4096]{2,1,0:T(8,128)(2,1)} %all_to_all.10) | copy-start | bytes 25165828
  155.4 7.2 %copy-start.3 = (bf16[1024,768]{1,0:T(8,128)(2,1)S(1)}, bf16[1024,768]{1,0:T(8,128)(2,1)}, u32[]{:S(2)}) copy-start(bf16[1024,768]{1,0:T(8,128)(2,1)} %get-tuple-element.22) | copy-start | bytes 4718596
  162.6 5.0 %copy-start.2 = (bf16[1024,768]{1,0:T(8,128)(2,1)S(1)}, bf16[1024,768]{1,0:T(8,128)(2,1)}, u32[]{:S(2)}) copy-start(bf16[1024,768]{1,0:T(8,128)(2,1)} %get-tuple-element.21) | copy-start | bytes 4718596

commit v2 on v1

v2 whole, which is shorter than its diff:
```python
import functools
import jax
import jax.numpy as jnp
from jax import lax
from jax.experimental import pallas as pl
from jax.experimental.pallas import tpu as pltpu
from jax.sharding import PartitionSpec as P

BF16 = jnp.bfloat16
F32 = jnp.float32
LAST_LAST = (((1,), (1,)), ((), ()))
FIRST_FIRST = (((0,), (0,)), ((), ()))
VMEM_LIMIT = 56 * 1024 * 1024


def iota(shape, dim):
    return lax.broadcasted_iota(jnp.int32, shape, dim)


def dot(a, b, dims=(((1,), (0,)), ((), ()))):
    return lax.dot_general(a, b, dims, preferred_element_type=F32)


def route_slots(ids, placement, cap):
    top, tokens = ids.shape
    experts = placement.shape[1]
    expert = iota((experts, tokens), 0)
    hits = [ids[k : k + 1, :] == expert for k in range(top)]
    named = functools.reduce(jnp.logical_or, hits)
    earlier = (iota((tokens, tokens), 0) < iota((tokens, tokens), 1)).astype(F32)
    count = dot(named.astype(F32).astype(BF16), earlier.astype(BF16)).astype(jnp.int32)
    diagonal = iota((experts, experts), 0) == iota((experts, experts), 1)
    serving = jnp.sum(jnp.where(diagonal, placement, 0), 1, keepdims=True)
    slot = serving * cap + count
    return jnp.concatenate(
        [jnp.sum(jnp.where(hit, slot, 0), 0, keepdims=True) for hit in hits], 0
    )


def selectors(slots, weights, first, rows):
    top, tokens = slots.shape
    row = iota((rows, tokens), 0) + first
    hits = [row == slots[k : k + 1, :] for k in range(top)]
    chosen = functools.reduce(jnp.logical_or, hits)
    weight = functools.reduce(
        jnp.add, [jnp.where(hits[k], weights[k : k + 1, :], 0.0) for k in range(top)]
    )
    high = weight.astype(BF16)
    low = (weight - high.astype(F32)).astype(BF16)
    return hits, chosen.astype(F32).astype(BF16), high, low


def slots_kernel(cap, ids_ref, placement_ref, weight_ref, tokens_ref, out_ref, slots_ref):
    rows = out_ref.shape[0]

    @pl.when(pl.program_id(0) == 0)
    def _():
        slots_ref[...] = route_slots(ids_ref[...], placement_ref[...], cap)

    _, chosen, _, _ = selectors(slots_ref[...], weight_ref[...], pl.program_id(0) * rows, rows)
    out_ref[...] = dot(chosen, tokens_ref[...]).astype(BF16)


def scaled_kernel(slots_ref, weight_ref, cot_ref, out_ref):
    rows = out_ref.shape[0]
    _, _, high, low = selectors(slots_ref[...], weight_ref[...], pl.program_id(0) * rows, rows)
    cot = cot_ref[...]
    out_ref[...] = (dot(high, cot) + dot(low, cot)).astype(BF16)


def whole(shape):
    return pl.BlockSpec(shape, lambda i: (0, 0))


def strip(block, width):
    return pl.BlockSpec((block, width), lambda i: (i, 0))


def columns(rows, block):
    return pl.BlockSpec((rows, block), lambda i: (0, i))


def params(limit=VMEM_LIMIT):
    return pltpu.CompilerParams(vmem_limit_bytes=limit)


def cost(flops, moved):
    return pl.CostEstimate(flops=flops, bytes_accessed=moved, transcendentals=0)


def pack_tokens(ids, placement, weights, tokens, cap):
    top, tok_dev = ids.shape
    experts = placement.shape[1]
    width = tokens.shape[1]
    total = experts * cap
    block = min(total, 256)
    return pl.pallas_call(
        functools.partial(slots_kernel, cap),
        grid=(total // block,),
        in_specs=[
            whole((top, tok_dev)),
            whole((1, experts)),
            whole((top, tok_dev)),
            whole((tok_dev, width)),
        ],
        out_specs=[strip(block, width), whole((top, tok_dev))],
        out_shape=[
            jax.ShapeDtypeStruct((total, width), BF16),
            jax.ShapeDtypeStruct((top, tok_dev), jnp.int32),
        ],
        compiler_params=params(),
        name="pack_tokens",
    )(ids, placement, weights, tokens)


def pack_scaled(slots, weights, cotangent, total):
    top, tok_dev = slots.shape
    width = cotangent.shape[1]
    block = min(total, 256)
    return pl.pallas_call(
        scaled_kernel,
        grid=(total // block,),
        in_specs=[whole((top, tok_dev)), whole((top, tok_dev)), whole((tok_dev, width))],
        out_specs=strip(block, width),
        out_shape=jax.ShapeDtypeStruct((total, width), BF16),
        compiler_params=params(),
        cost_estimate=cost(4 * total * tok_dev * width, 2 * total * width),
        name="pack_scaled",
    )(slots, weights, cotangent)


def forward_kernel(rows_ref, gate_ref, up_ref, down_ref, out_ref, gate_pre_ref, up_proj_ref, hidden_ref):
    inputs = rows_ref[...]
    gate_pre = dot(inputs, gate_ref[...])
    up_proj = dot(inputs, up_ref[...])
    gate_pre_ref[...] = gate_pre
    up_proj_ref[...] = up_proj
    hidden = (gate_pre * jax.nn.sigmoid(gate_pre) * up_proj).astype(BF16)
    hidden_ref[...] = hidden
    out_ref[...] = dot(hidden, down_ref[...]).astype(BF16)


def forward(rows, w_gate, w_up, w_down):
    total, width = rows.shape
    ff = w_gate.shape[1]
    block = min(total, 256)
    return pl.pallas_call(
        forward_kernel,
        grid=(total // block,),
        in_specs=[strip(block, width)] + [pl.BlockSpec(memory_space=pltpu.VMEM)] * 3,
        out_specs=[strip(block, width), strip(block, ff), strip(block, ff), strip(block, ff)],
        out_shape=[
            jax.ShapeDtypeStruct((total, width), BF16),
            jax.ShapeDtypeStruct((total, ff), F32),
            jax.ShapeDtypeStruct((total, ff), F32),
            jax.ShapeDtypeStruct((total, ff), BF16),
        ],
        compiler_params=params(),
        cost_estimate=cost(6 * total * width * ff, 4 * total * width + 6 * width * ff + 10 * total * ff),
        name="expert_forward",
    )(rows, w_gate, w_up, w_down)


def backward_kernel(rows_ref, gate_pre_ref, up_proj_ref, gate_ref, up_ref, down_ref, din_ref, dgate_ref, dup_ref):
    d_hidden = dot(rows_ref[...], down_ref[...], LAST_LAST)
    gate_pre = gate_pre_ref[...]
    sig = jax.nn.sigmoid(gate_pre)
    d_gate = (d_hidden * up_proj_ref[...] * sig * (1.0 + gate_pre * (1.0 - sig))).astype(BF16)
    d_up = (d_hidden * gate_pre * sig).astype(BF16)
    dgate_ref[...] = d_gate
    dup_ref[...] = d_up
    din_ref[...] = (
        dot(d_gate, gate_ref[...], LAST_LAST) + dot(d_up, up_ref[...], LAST_LAST)
    ).astype(BF16)


def backward(rows, gate_pre, up_proj, w_gate, w_up, w_down):
    total, width = rows.shape
    ff = w_gate.shape[1]
    block = min(total, 256)
    return pl.pallas_call(
        backward_kernel,
        grid=(total // block,),
        in_specs=[strip(block, width), strip(block, ff), strip(block, ff)]
        + [pl.BlockSpec(memory_space=pltpu.VMEM)] * 3,
        out_specs=[strip(block, width), strip(block, ff), strip(block, ff)],
        out_shape=[
            jax.ShapeDtypeStruct((total, width), BF16),
            jax.ShapeDtypeStruct((total, ff), BF16),
            jax.ShapeDtypeStruct((total, ff), BF16),
        ],
        compiler_params=params(),
        cost_estimate=cost(6 * total * width * ff, 4 * total * width + 6 * width * ff + 12 * total * ff),
        name="expert_backward",
    )(rows, gate_pre, up_proj, w_gate, w_up, w_down)


def mixed_kernel(slots_ref, weight_ref, cot_ref, out_ref, mixed_ref, groute_ref, sel_ref, dots_ref):
    step = pl.program_id(0)
    total = out_ref.shape[0]
    tok_dev = cot_ref.shape[0]
    top = slots_ref.shape[0]

    @pl.when(step == 0)
    def _():
        _, _, high, low = selectors(slots_ref[...], weight_ref[...], 0, total)
        sel_ref[:, :tok_dev] = high
        sel_ref[:, tok_dev:] = low
        dots_ref[...] = jnp.zeros_like(dots_ref)

    outcome = out_ref[...]
    halves = dot(sel_ref[...], outcome, FIRST_FIRST)
    mixed_ref[...] = (halves[:tok_dev] + halves[tok_dev:]).astype(BF16)
    dots_ref[...] += dot(outcome, cot_ref[...], LAST_LAST)

    @pl.when(step == pl.num_programs(0) - 1)
    def _():
        slots = slots_ref[...]
        row = iota((total, tok_dev), 0)
        dots = dots_ref[...]
        groute_ref[...] = jnp.concatenate(
            [
                jnp.sum(jnp.where(row == slots[k : k + 1, :], dots, 0.0), 0, keepdims=True)
                for k in range(top)
            ],
            0,
        )


def unpack_mixed(slots, weights, cotangent, outcome):
    top, tok_dev = slots.shape
    total, width = outcome.shape
    block = min(width, 512)
    return pl.pallas_call(
        mixed_kernel,
        grid=(width // block,),
        in_specs=[
            whole((top, tok_dev)),
            whole((top, tok_dev)),
            columns(tok_dev, block),
            columns(total, block),
        ],
        out_specs=[columns(tok_dev, block), whole((top, tok_dev))],
        out_shape=[
            jax.ShapeDtypeStruct((tok_dev, width), BF16),
            jax.ShapeDtypeStruct((top, tok_dev), F32),
        ],
        scratch_shapes=[
            pltpu.VMEM((total, 2 * tok_dev), BF16),
            pltpu.VMEM((total, tok_dev), F32),
        ],
        compiler_params=params(),
        cost_estimate=cost(6 * total * tok_dev * width, 2 * total * width),
        name="unpack_mixed",
    )(slots, weights, cotangent, outcome)


def gtok_kernel(slots_ref, din_ref, gtok_ref, sel_ref):
    total = din_ref.shape[0]

    @pl.when(pl.program_id(0) == 0)
    def _():
        slots = slots_ref[...]
        row = iota((total, slots.shape[1]), 0)
        hits = [row == slots[k : k + 1, :] for k in range(slots.shape[0])]
        sel_ref[...] = functools.reduce(jnp.logical_or, hits).astype(F32).astype(BF16)

    gtok_ref[...] = dot(sel_ref[...], din_ref[...], FIRST_FIRST).astype(BF16)


def unpack_tokens(slots, d_inputs):
    top, tok_dev = slots.shape
    total, width = d_inputs.shape
    block = min(width, 512)
    return pl.pallas_call(
        gtok_kernel,
        grid=(width // block,),
        in_specs=[whole((top, tok_dev)), columns(total, block)],
        out_specs=columns(tok_dev, block),
        out_shape=jax.ShapeDtypeStruct((tok_dev, width), BF16),
        scratch_shapes=[pltpu.VMEM((total, tok_dev), BF16)],
        compiler_params=params(),
        cost_estimate=cost(2 * total * tok_dev * width, 2 * total * width),
        name="unpack_tokens",
    )(slots, d_inputs)


def exchange(buffer, experts):
    total, width = buffer.shape
    moved = lax.all_to_all(
        buffer.reshape(experts, total // experts, width),
        ("col", "row"),
        split_axis=0,
        concat_axis=0,
        tiled=True,
    )
    return moved.reshape(total, width)


def per_device(tokens, route_weight, expert_ids, placement, w_gate, w_up, w_down, cotangent):
    tok_dev, width = tokens.shape
    fan_out = expert_ids.shape[1]
    experts = placement.shape[0]
    cap = max(2, min(tok_dev // 2, 8 * max(1, tok_dev * fan_out // (8 * experts))))
    weights = route_weight.T
    gate, up, down = w_gate[0], w_up[0], w_down[0]
    packed, slots = pack_tokens(
        expert_ids.T, placement.reshape(1, experts), weights, tokens, cap
    )
    inputs = exchange(packed, experts)
    scaled = exchange(pack_scaled(slots, weights, cotangent, experts * cap), experts)
    outcome, gate_pre, up_proj, hidden = forward(inputs, gate, up, down)
    outcome = exchange(outcome, experts)
    d_inputs, d_gate, d_up = backward(scaled, gate_pre, up_proj, gate, up, down)
    returned = exchange(d_inputs, experts)
    grad_gate = dot(inputs, d_gate, FIRST_FIRST).astype(BF16)
    grad_up = dot(inputs, d_up, FIRST_FIRST).astype(BF16)
    grad_down = dot(hidden, scaled, FIRST_FIRST).astype(BF16)
    mixed, grad_route = unpack_mixed(slots, weights, cotangent, outcome)
    grad_tokens = unpack_tokens(slots, returned)
    return (mixed, grad_tokens, grad_route.T, grad_gate[None], grad_up[None], grad_down[None])


def solution(mesh):
    split = P(("col", "row"), None)
    split3 = P(("col", "row"), None, None)
    return jax.shard_map(
        per_device,
        mesh=mesh,
        in_specs=(split, split, split, P(), split3, split3, split3, split),
        out_specs=(split, split, split, split3, split3, split3),
        check_vma=False,
    )
```

time: 270 us -> 251 us (0.930)
  blocking collectives: 110 us -> 0 us
  waiting for transfers between devices: 89.1 us -> 141 us
  starting transfers between devices: 8.1 us -> 30.1 us
  Pallas kernels: 44.4 us -> 56.2 us
  matrix products: 17.1 us -> 22 us
    all_to_all x1 -> x0, blocking collectives: 110 us -> none  [exchange(): lax.all_to_all(buffer.reshape(experts, total // experts, width), ('col',...]
    all_to_all x1 -> x4, waiting for transfers between devices: 89.1 us -> 141 us  [exchange(): lax.all_to_all(buffer.reshape(experts, total // experts, width), ('col',...]
    all_to_all x1 -> x4, starting transfers between devices: 8.1 us -> 30.1 us  [exchange(): lax.all_to_all(buffer.reshape(experts, total // experts, width), ('col',...]
    pallas_call x3 -> x6, Pallas kernels: 44.4 us -> 56.2 us  [the longest x1 19.8 us: backward(): pl.pallas_call(backward_kernel, grid=(total // block,), in_specs=[strip(b...]
    dot_general x3, matrix products: 17.1 us -> 22 us  [dot(): return lax.dot_general(a, b, dims, preferred_element_type=F32)]
  transfers between devices with their start and end apart: 1 -> 4, of which waited for: 1 -> 4; matrix products, arithmetic and copies ran while one was open for 6% -> 9% of each run, Pallas kernels for 0% -> 19%
where the time goes in v2:
time: 251 us; the launch traced here: 250 us
  waiting for transfers between devices  141 us (56%)
  Pallas kernels  56.2 us (22%)
  starting transfers between devices  30.1 us (12%)
  matrix products  22 us (9%)
    all_to_all x4, waiting for transfers between devices, exchange(): lax.all_to_all(buffer.reshape(experts, total // experts, width), ('col',...  141 us
    all_to_all x4, starting transfers between devices, exchange(): lax.all_to_all(buffer.reshape(experts, total // experts, width), ('col',...  30.1 us
    dot_general x3, matrix products, dot(): return lax.dot_general(a, b, dims, preferred_element_type=F32)  22 us
    pallas_call x1, Pallas kernels, backward(): pl.pallas_call(backward_kernel, grid=(total // block,), in_specs=[strip(b...  19.8 us
    pallas_call x1, Pallas kernels, forward(): pl.pallas_call(forward_kernel, grid=(total // block,), in_specs=[strip(bl...  15.6 us
    pallas_call x1, Pallas kernels, unpack_mixed(): pl.pallas_call(mixed_kernel, grid=(width // block,), in_specs=[whole((top...  6.22 us
    pallas_call x1, Pallas kernels, pack_scaled(): pl.pallas_call(scaled_kernel, grid=(total // block,), in_specs=[whole((to...  5.28 us
  transfers between devices with their start and end apart: 4, of which 4 were waited for; matrix products, arithmetic and copies ran while one was open for 9% of the time, Pallas kernels for 19%

profile of v2, /device:TPU:1, one launch (start us, length us, event | category | flops | bytes accessed | tf_op | source)
XLA Modules:
  0.0 250.3 jit_solution(3398204140819470610)
XLA Ops:
  0.6 4.6 %pack_tokens.1 = (bf16[1024,2048]{1,0:T(8,128)(2,1)}, s32[4,128]{1,0:T(4,128)}) custom-call(s32[4,128]{1,0:T(4,128)} %bitcast.37, s32[1,128]{1,0:T(1,128)} %bitcast.38, f32[4,128]{1,0:T(4,128)} %bitcast.34, bf16[128,2048]{1,0:T(8,128)(2,1)} %tokens_ref.1), custom_call_target="tpu_custom_call" | custom-call | tf_op jit(solution)/shard_map/pack_tokens/pallas_call | solution.py:97
  5.3 12.0 %all-to-all-start = ((bf16[128,8,2048]{2,1,0:T(8,128)(2,1)}), bf16[128,8,2048]{2,1,0:T(8,128)(2,1)}, u32[]{:S(2)}, u32[]{:S(2)}) async-start(bf16[128,8,2048]{2,1,0:T(8,128)(2,1)} %bitcast.33), calls=%async_computation | async-start | bytes 8388608 | tf_op jit(solution)/shard_map/all_to_all | solution.py:290
  17.2 5.3 %pack_scaled.1 = bf16[1024,2048]{1,0:T(8,128)(2,1)} custom-call(s32[4,128]{1,0:T(4,128)} %get-tuple-element.17.slots_ref, f32[4,128]{1,0:T(4,128)} %bitcast.35, bf16[128,2048]{1,0:T(8,128)(2,1)} %cot_ref.3), custom_call_target="tpu_custom_call" | custom-call | flops 1073741824 | bytes 4194304 | tf_op jit(solution)/shard_map/pack_scaled/pallas_call | solution.py:120
  22.5 47.3 %all-to-all-done = bf16[128,8,2048]{2,1,0:T(8,128)(2,1)} async-done(((bf16[128,8,2048]{2,1,0:T(8,128)(2,1)}), bf16[128,8,2048]{2,1,0:T(8,128)(2,1)}, u32[]{:S(2)}, u32[]{:S(2)}) %all-to-all-start) | async-done | bytes 4194336 | tf_op jit(solution)/shard_map/all_to_all | solution.py:290
  69.8 6.0 %all-to-all-start.2 = ((bf16[128,8,2048]{2,1,0:T(8,128)(2,1)}), bf16[128,8,2048]{2,1,0:T(8,128)(2,1)}, u32[]{:S(2)}, u32[]{:S(2)}) async-start(bf16[128,8,2048]{2,1,0:T(8,128)(2,1)} %bitcast.30), calls=%async_computation.2 | async-start | bytes 8388608 | tf_op jit(solution)/shard_map/all_to_all | solution.py:290
  75.8 15.6 %expert_forward.1 = (bf16[1024,2048]{1,0:T(8,128)(2,1)}, f32[1024,768]{1,0:T(8,128)}, f32[1024,768]{1,0:T(8,128)}, bf16[1024,768]{1,0:T(8,128)(2,1)}) custom-call(bf16[1024,2048]{1,0:T(8,128)(2,1)} %bitcast.4.rows_ref, bf16[2048,768]{1,0:T(8,128)(2,1)} %bitcast.39, bf16[2048,768]{1,0:T(8,128)(2,1)} %bitcast.41, bf16[768,2048]{1,0:T(8,128)(2,1)} %bitcast.43), custom_call_target="tpu_custom_call" | custom-call | flops 9663676416 | bytes 25690112 | tf_op jit(solution)/shard_map/expert_forward/pallas_call | solution.py:147
  91.4 36.9 %all-to-all-done.2 = bf16[128,8,2048]{2,1,0:T(8,128)(2,1)} async-done(((bf16[128,8,2048]{2,1,0:T(8,128)(2,1)}), bf16[128,8,2048]{2,1,0:T(8,128)(2,1)}, u32[]{:S(2)}, u32[]{:S(2)}) %all-to-all-start.2) | async-done | bytes 4194336 | tf_op jit(solution)/shard_map/all_to_all | solution.py:290
  128.3 6.0 %all-to-all-start.1 = ((bf16[128,8,2048]{2,1,0:T(8,128)(2,1)}), bf16[128,8,2048]{2,1,0:T(8,128)(2,1)}, u32[]{:S(2)}, u32[]{:S(2)}) async-start(bf16[128,8,2048]{2,1,0:T(8,128)(2,1)} %bitcast.32), calls=%async_computation.1 | async-start | bytes 8388608 | tf_op jit(solution)/shard_map/all_to_all | solution.py:290
  134.4 19.8 %expert_backward.1 = (bf16[1024,2048]{1,0:T(8,128)(2,1)}, bf16[1024,768]{1,0:T(8,128)(2,1)}, bf16[1024,768]{1,0:T(8,128)(2,1)}) custom-call(bf16[1024,2048]{1,0:T(8,128)(2,1)} %bitcast.11.rows_ref, f32[1024,768]{1,0:T(8,128)} %get-tuple-element.21.gate_pre_ref, f32[1024,768]{1,0:T(8,128)} %get-tuple-element.22.up_proj_ref, bf16[2048,768]{1,0:T(8,128)(2,1)} %bitcast.40, ...), custom_call_target="tpu_custom_call" | custom-call | flops 9663676416 | bytes 27262976 | tf_op jit(solution)/shard_map/expert_backward/pallas_call | solution.py:181
  154.2 32.8 %all-to-all-done.1 = bf16[128,8,2048]{2,1,0:T(8,128)(2,1)} async-done(((bf16[128,8,2048]{2,1,0:T(8,128)(2,1)}), bf16[128,8,2048]{2,1,0:T(8,128)(2,1)}, u32[]{:S(2)}, u32[]{:S(2)}) %all-to-all-start.1) | async-done | bytes 4194336 | tf_op jit(solution)/shard_map/all_to_all | solution.py:290
  186.9 0.0 copy-start.2
  186.9 6.1 %all-to-all-start.3 = ((bf16[128,8,2048]{2,1,0:T(8,128)(2,1)}), bf16[128,8,2048]{2,1,0:T(8,128)(2,1)}, u32[]{:S(2)}, u32[]{:S(2)}) async-start(bf16[128,8,2048]{2,1,0:T(8,128)(2,1)} %bitcast.31), calls=%async_computation.3 | async-start | bytes 8388608 | tf_op jit(solution)/shard_map/all_to_all | solution.py:290
  193.0 0.0 copy-done.2
  193.0 0.0 copy-start.1
  193.0 7.5 %fusion = bf16[1,2048,768]{2,1,0:T(8,128)(2,1)} fusion(bf16[1024,768]{1,0:T(8,128)(2,1)S(1)} %copy-done.2, bf16[128,8,2048]{2,1,0:T(8,128)(2,1)} %all-to-all-done), kind=kOutput, calls=%fused_computation.3 | convolution fusion | flops 3222798336 | bytes 8912896 | tf_op jit(solution)/shard_map/dot_general | solution.py:21
  200.5 0.0 copy-done.1
  200.5 0.0 copy-start
  200.5 7.5 %fusion.1 = bf16[1,2048,768]{2,1,0:T(8,128)(2,1)} fusion(bf16[1024,768]{1,0:T(8,128)(2,1)S(1)} %copy-done.1, bf16[128,8,2048]{2,1,0:T(8,128)(2,1)} %all-to-all-done), kind=kOutput, calls=%fused_computation.4 | convolution fusion | flops 3222798336 | bytes 8912896 | tf_op jit(solution)/shard_map/dot_general | solution.py:21
  208.0 0.0 copy-done
  208.0 7.0 %fusion.2 = bf16[1,768,2048]{2,1,0:T(8,128)(2,1)} fusion(bf16[1024,768]{1,0:T(8,128)(2,1)S(1)} %copy-done, bf16[128,8,2048]{2,1,0:T(8,128)(2,1)} %all-to-all-done.2), kind=kOutput, calls=%fused_computation.5 | convolution fusion | flops 3222798336 | bytes 8912896 | tf_op jit(solution)/shard_map/dot_general | solution.py:21
  215.1 6.2 %unpack_mixed.1 = (bf16[128,2048]{1,0:T(8,128)(2,1)}, f32[4,128]{1,0:T(4,128)}) custom-call(s32[4,128]{1,0:T(4,128)} %get-tuple-element.17.slots_ref, f32[4,128]{1,0:T(4,128)} %bitcast.36, bf16[128,2048]{1,0:T(8,128)(2,1)} %cot_ref.3, bf16[1024,2048]{1,0:T(8,128)(2,1)} %bitcast.9.out_ref), custom_call_target="tpu_custom_call" | custom-call | flops 1610612736 | bytes 4194304 | tf_op jit(solution)/shard_map/unpack_mixed/pallas_call | solution.py:234
  221.3 24.3 %all-to-all-done.3 = bf16[128,8,2048]{2,1,0:T(8,128)(2,1)} async-done(((bf16[128,8,2048]{2,1,0:T(8,128)(2,1)}), bf16[128,8,2048]{2,1,0:T(8,128)(2,1)}, u32[]{:S(2)}, u32[]{:S(2)}) %all-to-all-start.3) | async-done | bytes 4194336 | tf_op jit(solution)/shard_map/all_to_all | solution.py:290
  245.6 4.7 %unpack_tokens.1 = bf16[128,2048]{1,0:T(8,128)(2,1)} custom-call(s32[4,128]{1,0:T(4,128)} %get-tuple-element.17.slots_ref, bf16[1024,2048]{1,0:T(8,128)(2,1)} %bitcast.13.din_ref), custom_call_target="tpu_custom_call" | custom-call | flops 536870912 | bytes 4194304 | tf_op jit(solution)/shard_map/unpack_tokens/pallas_call | solution.py:275
Async XLA Ops:
  5.3 64.5 %all-to-all-start = ((bf16[128,8,2048]{2,1,0:T(8,128)(2,1)}), bf16[128,8,2048]{2,1,0:T(8,128)(2,1)}, u32[]{:S(2)}, u32[]{:S(2)}) async-start(bf16[128,8,2048]{2,1,0:T(8,128)(2,1)} %bitcast.33), calls=%async_computation | async-start | bytes 8388608 | tf_op jit(solution)/shard_map/all_to_all | solution.py:290
  69.8 58.6 %all-to-all-start.2 = ((bf16[128,8,2048]{2,1,0:T(8,128)(2,1)}), bf16[128,8,2048]{2,1,0:T(8,128)(2,1)}, u32[]{:S(2)}, u32[]{:S(2)}) async-start(bf16[128,8,2048]{2,1,0:T(8,128)(2,1)} %bitcast.30), calls=%async_computation.2 | async-start | bytes 8388608 | tf_op jit(solution)/shard_map/all_to_all | solution.py:290
  128.3 58.6 %all-to-all-start.1 = ((bf16[128,8,2048]{2,1,0:T(8,128)(2,1)}), bf16[128,8,2048]{2,1,0:T(8,128)(2,1)}, u32[]{:S(2)}, u32[]{:S(2)}) async-start(bf16[128,8,2048]{2,1,0:T(8,128)(2,1)} %bitcast.32), calls=%async_computation.1 | async-start | bytes 8388608 | tf_op jit(solution)/shard_map/all_to_all | solution.py:290
  186.9 6.1 %copy-start.2 = (bf16[1024,768]{1,0:T(8,128)(2,1)S(1)}, bf16[1024,768]{1,0:T(8,128)(2,1)}, u32[]{:S(2)}) copy-start(bf16[1024,768]{1,0:T(8,128)(2,1)} %get-tuple-element.25) | copy-start | bytes 4718596
  186.9 58.6 %all-to-all-start.3 = ((bf16[128,8,2048]{2,1,0:T(8,128)(2,1)}), bf16[128,8,2048]{2,1,0:T(8,128)(2,1)}, u32[]{:S(2)}, u32[]{:S(2)}) async-start(bf16[128,8,2048]{2,1,0:T(8,128)(2,1)} %bitcast.31), calls=%async_computation.3 | async-start | bytes 8388608 | tf_op jit(solution)/shard_map/all_to_all | solution.py:290
  193.0 7.5 %copy-start.1 = (bf16[1024,768]{1,0:T(8,128)(2,1)S(1)}, bf16[1024,768]{1,0:T(8,128)(2,1)}, u32[]{:S(2)}) copy-start(bf16[1024,768]{1,0:T(8,128)(2,1)} %get-tuple-element.26) | copy-start | bytes 4718596
  200.5 7.5 %copy-start = (bf16[1024,768]{1,0:T(8,128)(2,1)S(1)}, bf16[1024,768]{1,0:T(8,128)(2,1)}, u32[]{:S(2)}) copy-start(bf16[1024,768]{1,0:T(8,128)(2,1)} %get-tuple-element.27) | copy-start | bytes 4718596

commit v3 on v2

--- a/solution.py
+++ b/solution.py
@@ -11,6 +11,8 @@
 LAST_LAST = (((1,), (1,)), ((), ()))
 FIRST_FIRST = (((0,), (0,)), ((), ()))
 VMEM_LIMIT = 56 * 1024 * 1024
+PACK_CHUNKS = 4
+UNPACK_CHUNKS = 4
 
 
 def iota(shape, dim):
@@ -37,6 +39,12 @@
     )
 
 
+def hits_of(slots, first, rows):
+    row = iota((rows, slots.shape[1]), 0) + first
+    hits = [row == slots[k : k + 1, :] for k in range(slots.shape[0])]
+    return jnp.where(functools.reduce(jnp.logical_or, hits), 1.0, 0.0).astype(BF16)
+
+
 def selectors(slots, weights, first, rows):
     top, tokens = slots.shape
     row = iota((rows, tokens), 0) + first
@@ -50,15 +58,20 @@
     return hits, chosen.astype(F32).astype(BF16), high, low
 
 
-def slots_kernel(cap, ids_ref, placement_ref, weight_ref, tokens_ref, out_ref, slots_ref):
-    rows = out_ref.shape[0]
-
-    @pl.when(pl.program_id(0) == 0)
-    def _():
-        slots_ref[...] = route_slots(ids_ref[...], placement_ref[...], cap)
-
-    _, chosen, _, _ = selectors(slots_ref[...], weight_ref[...], pl.program_id(0) * rows, rows)
-    out_ref[...] = dot(chosen, tokens_ref[...]).astype(BF16)
+def slots_kernel(cap, chunks, ids_ref, placement_ref, tokens_ref, out_ref, slots_ref, rows_ref, sems):
+    size = rows_ref.shape[1]
+    slots = route_slots(ids_ref[...], placement_ref[...], cap)
+    slots_ref[...] = slots
+    copies = []
+    for i in range(chunks):
+        chosen = hits_of(slots, i * size, size)
+        rows_ref[i] = dot(chosen, tokens_ref[...]).astype(BF16)
+        copies.append(
+            pltpu.make_async_copy(rows_ref.at[i], out_ref.at[pl.ds(i * size, size)], sems.at[i])
+        )
+        copies[-1].start()
+    for copy in copies:
+        copy.wait()
 
 
 def scaled_kernel(slots_ref, weight_ref, cot_ref, out_ref):
@@ -88,29 +101,27 @@
     return pl.CostEstimate(flops=flops, bytes_accessed=moved, transcendentals=0)
 
 
-def pack_tokens(ids, placement, weights, tokens, cap):
+def pack_tokens(ids, placement, tokens, cap, chunks=PACK_CHUNKS):
     top, tok_dev = ids.shape
     experts = placement.shape[1]
     width = tokens.shape[1]
     total = experts * cap
-    block = min(total, 256)
-    return pl.pallas_call(
-        functools.partial(slots_kernel, cap),
-        grid=(total // block,),
-        in_specs=[
-            whole((top, tok_dev)),
-            whole((1, experts)),
-            whole((top, tok_dev)),
-            whole((tok_dev, width)),
-        ],
-        out_specs=[strip(block, width), whole((top, tok_dev))],
+    in_vmem = pl.BlockSpec(memory_space=pltpu.VMEM)
+    return pl.pallas_call(
+        functools.partial(slots_kernel, cap, chunks),
+        in_specs=[in_vmem] * 3,
+        out_specs=[pl.BlockSpec(memory_space=pl.ANY), in_vmem],
         out_shape=[
             jax.ShapeDtypeStruct((total, width), BF16),
             jax.ShapeDtypeStruct((top, tok_dev), jnp.int32),
         ],
+        scratch_shapes=[
+            pltpu.VMEM((chunks, total // chunks, width), BF16),
+            pltpu.SemaphoreType.DMA((chunks,)),
+        ],
         compiler_params=params(),
         name="pack_tokens",
-    )(ids, placement, weights, tokens)
+    )(ids, placement, tokens)
 
 
 def pack_scaled(slots, weights, cotangent, total):
@@ -255,30 +266,47 @@
     )(slots, weights, cotangent, outcome)
 
 
-def gtok_kernel(slots_ref, din_ref, gtok_ref, sel_ref):
-    total = din_ref.shape[0]
-
-    @pl.when(pl.program_id(0) == 0)
-    def _():
-        slots = slots_ref[...]
-        row = iota((total, slots.shape[1]), 0)
-        hits = [row == slots[k : k + 1, :] for k in range(slots.shape[0])]
-        sel_ref[...] = functools.reduce(jnp.logical_or, hits).astype(F32).astype(BF16)
-
-    gtok_ref[...] = dot(sel_ref[...], din_ref[...], FIRST_FIRST).astype(BF16)
-
-
-def unpack_tokens(slots, d_inputs):
-    top, tok_dev = slots.shape
+def gtok_kernel(chunks, slots_ref, din_ref, gtok_ref, rows_ref, part_ref, in_sems, out_sems):
+    total, width = din_ref.shape
+    size = width // chunks
+    arrivals = []
+    for i in range(chunks):
+        arrivals.append(
+            pltpu.make_async_copy(
+                din_ref.at[:, pl.ds(i * size, size)], rows_ref.at[i], in_sems.at[i]
+            )
+        )
+        arrivals[-1].start()
+    chosen = hits_of(slots_ref[...], 0, total).T
+    leaving = []
+    for i in range(chunks):
+        arrivals[i].wait()
+        part_ref[i] = dot(chosen, rows_ref[i]).astype(BF16)
+        leaving.append(
+            pltpu.make_async_copy(
+                part_ref.at[i], gtok_ref.at[:, pl.ds(i * size, size)], out_sems.at[i]
+            )
+        )
+        leaving[-1].start()
+    for copy in leaving:
+        copy.wait()
+
+
+def unpack_tokens(slots, d_inputs, chunks=UNPACK_CHUNKS):
+    tok_dev = slots.shape[1]
     total, width = d_inputs.shape
-    block = min(width, 512)
-    return pl.pallas_call(
-        gtok_kernel,
-        grid=(width // block,),
-        in_specs=[whole((top, tok_dev)), columns(total, block)],
-        out_specs=columns(tok_dev, block),
+    anywhere = pl.BlockSpec(memory_space=pl.ANY)
+    return pl.pallas_call(
+        functools.partial(gtok_kernel, chunks),
+        in_specs=[pl.BlockSpec(memory_space=pltpu.VMEM), anywhere],
+        out_specs=anywhere,
         out_shape=jax.ShapeDtypeStruct((tok_dev, width), BF16),
-        scratch_shapes=[pltpu.VMEM((total, tok_dev), BF16)],
+        scratch_shapes=[
+            pltpu.VMEM((chunks, total, width // chunks), BF16),
+            pltpu.VMEM((chunks, tok_dev, width // chunks), BF16),
+            pltpu.SemaphoreType.DMA((chunks,)),
+            pltpu.SemaphoreType.DMA((chunks,)),
+        ],
         compiler_params=params(),
         cost_estimate=cost(2 * total * tok_dev * width, 2 * total * width),
         name="unpack_tokens",
@@ -305,7 +333,7 @@
     weights = route_weight.T
     gate, up, down = w_gate[0], w_up[0], w_down[0]
     packed, slots = pack_tokens(
-        expert_ids.T, placement.reshape(1, experts), weights, tokens, cap
+        expert_ids.T, placement.reshape(1, experts), tokens, cap
     )
     inputs = exchange(packed, experts)
     scaled = exchange(pack_scaled(slots, weights, cotangent, experts * cap), experts)

time: 251 us -> 250 us (level)
  no operation moved by 1% of the time
where the time goes in v3:
time: 250 us; the launch traced here: 249 us
  waiting for transfers between devices  141 us (56%)
  Pallas kernels  55 us (22%)
  starting transfers between devices  30.1 us (12%)
  matrix products  22 us (9%)
    all_to_all x4, waiting for transfers between devices, exchange(): lax.all_to_all(buffer.reshape(experts, total // experts, width), ('col',...  141 us
    all_to_all x4, starting transfers between devices, exchange(): lax.all_to_all(buffer.reshape(experts, total // experts, width), ('col',...  30.1 us
    dot_general x3, matrix products, dot(): return lax.dot_general(a, b, dims, preferred_element_type=F32)  22 us
    pallas_call x1, Pallas kernels, backward(): pl.pallas_call(backward_kernel, grid=(total // block,), in_specs=[strip(b...  19.7 us
    pallas_call x1, Pallas kernels, forward(): pl.pallas_call(forward_kernel, grid=(total // block,), in_specs=[strip(bl...  15.6 us
    pallas_call x1, Pallas kernels, unpack_mixed(): pl.pallas_call(mixed_kernel, grid=(width // block,), in_specs=[whole((top...  6.21 us
    pallas_call x1, Pallas kernels, pack_scaled(): pl.pallas_call(scaled_kernel, grid=(total // block,), in_specs=[whole((to...  5.28 us
  transfers between devices with their start and end apart: 4, of which 4 were waited for; matrix products, arithmetic and copies ran while one was open for 9% of the time, Pallas kernels for 19%

profile of v3, /device:TPU:1, one launch (start us, length us, event | category | flops | bytes accessed | tf_op | source)
XLA Modules:
  0.0 249.3 jit_solution(3979169807025509653)
XLA Ops:
  0.6 4.3 %pack_tokens.1 = (bf16[1024,2048]{1,0:T(8,128)(2,1)}, s32[4,128]{1,0:T(4,128)}) custom-call(s32[4,128]{1,0:T(4,128)} %bitcast.34, s32[1,128]{1,0:T(1,128)} %bitcast.37, bf16[128,2048]{1,0:T(8,128)(2,1)} %tokens_ref.1), custom_call_target="tpu_custom_call" | custom-call | tf_op jit(solution)/shard_map/pack_tokens/pallas_call | solution.py:110
  4.9 12.0 %all-to-all-start = ((bf16[128,8,2048]{2,1,0:T(8,128)(2,1)}), bf16[128,8,2048]{2,1,0:T(8,128)(2,1)}, u32[]{:S(2)}, u32[]{:S(2)}) async-start(bf16[128,8,2048]{2,1,0:T(8,128)(2,1)} %bitcast.33), calls=%async_computation | async-start | bytes 8388608 | tf_op jit(solution)/shard_map/all_to_all | solution.py:318
  16.9 5.3 %pack_scaled.1 = bf16[1024,2048]{1,0:T(8,128)(2,1)} custom-call(s32[4,128]{1,0:T(4,128)} %get-tuple-element.17.slots_ref, f32[4,128]{1,0:T(4,128)} %bitcast.35, bf16[128,2048]{1,0:T(8,128)(2,1)} %cot_ref.3), custom_call_target="tpu_custom_call" | custom-call | flops 1073741824 | bytes 4194304 | tf_op jit(solution)/shard_map/pack_scaled/pallas_call | solution.py:131
  22.2 47.3 %all-to-all-done = bf16[128,8,2048]{2,1,0:T(8,128)(2,1)} async-done(((bf16[128,8,2048]{2,1,0:T(8,128)(2,1)}), bf16[128,8,2048]{2,1,0:T(8,128)(2,1)}, u32[]{:S(2)}, u32[]{:S(2)}) %all-to-all-start) | async-done | bytes 4194336 | tf_op jit(solution)/shard_map/all_to_all | solution.py:318
  69.4 6.0 %all-to-all-start.2 = ((bf16[128,8,2048]{2,1,0:T(8,128)(2,1)}), bf16[128,8,2048]{2,1,0:T(8,128)(2,1)}, u32[]{:S(2)}, u32[]{:S(2)}) async-start(bf16[128,8,2048]{2,1,0:T(8,128)(2,1)} %bitcast.30), calls=%async_computation.2 | async-start | bytes 8388608 | tf_op jit(solution)/shard_map/all_to_all | solution.py:318
  75.5 15.6 %expert_forward.1 = (bf16[1024,2048]{1,0:T(8,128)(2,1)}, f32[1024,768]{1,0:T(8,128)}, f32[1024,768]{1,0:T(8,128)}, bf16[1024,768]{1,0:T(8,128)(2,1)}) custom-call(bf16[1024,2048]{1,0:T(8,128)(2,1)} %bitcast.4.rows_ref, bf16[2048,768]{1,0:T(8,128)(2,1)} %bitcast.38, bf16[2048,768]{1,0:T(8,128)(2,1)} %bitcast.40, bf16[768,2048]{1,0:T(8,128)(2,1)} %bitcast.42), custom_call_target="tpu_custom_call" | custom-call | flops 9663676416 | bytes 25690112 | tf_op jit(solution)/shard_map/expert_forward/pallas_call | solution.py:158
  91.1 36.9 %all-to-all-done.2 = bf16[128,8,2048]{2,1,0:T(8,128)(2,1)} async-done(((bf16[128,8,2048]{2,1,0:T(8,128)(2,1)}), bf16[128,8,2048]{2,1,0:T(8,128)(2,1)}, u32[]{:S(2)}, u32[]{:S(2)}) %all-to-all-start.2) | async-done | bytes 4194336 | tf_op jit(solution)/shard_map/all_to_all | solution.py:318
  128.0 6.0 %all-to-all-start.1 = ((bf16[128,8,2048]{2,1,0:T(8,128)(2,1)}), bf16[128,8,2048]{2,1,0:T(8,128)(2,1)}, u32[]{:S(2)}, u32[]{:S(2)}) async-start(bf16[128,8,2048]{2,1,0:T(8,128)(2,1)} %bitcast.32), calls=%async_computation.1 | async-start | bytes 8388608 | tf_op jit(solution)/shard_map/all_to_all | solution.py:318
  134.1 19.7 %expert_backward.1 = (bf16[1024,2048]{1,0:T(8,128)(2,1)}, bf16[1024,768]{1,0:T(8,128)(2,1)}, bf16[1024,768]{1,0:T(8,128)(2,1)}) custom-call(bf16[1024,2048]{1,0:T(8,128)(2,1)} %bitcast.11.rows_ref, f32[1024,768]{1,0:T(8,128)} %get-tuple-element.21.gate_pre_ref, f32[1024,768]{1,0:T(8,128)} %get-tuple-element.22.up_proj_ref, bf16[2048,768]{1,0:T(8,128)(2,1)} %bitcast.39, ...), custom_call_target="tpu_custom_call" | custom-call | flops 9663676416 | bytes 27262976 | tf_op jit(solution)/shard_map/expert_backward/pallas_call | solution.py:192
  153.8 32.8 %all-to-all-done.1 = bf16[128,8,2048]{2,1,0:T(8,128)(2,1)} async-done(((bf16[128,8,2048]{2,1,0:T(8,128)(2,1)}), bf16[128,8,2048]{2,1,0:T(8,128)(2,1)}, u32[]{:S(2)}, u32[]{:S(2)}) %all-to-all-start.1) | async-done | bytes 4194336 | tf_op jit(solution)/shard_map/all_to_all | solution.py:318
  186.6 0.0 copy-start.2
  186.6 6.1 %all-to-all-start.3 = ((bf16[128,8,2048]{2,1,0:T(8,128)(2,1)}), bf16[128,8,2048]{2,1,0:T(8,128)(2,1)}, u32[]{:S(2)}, u32[]{:S(2)}) async-start(bf16[128,8,2048]{2,1,0:T(8,128)(2,1)} %bitcast.31), calls=%async_computation.3 | async-start | bytes 8388608 | tf_op jit(solution)/shard_map/all_to_all | solution.py:318
  192.7 0.0 copy-done.2
  192.7 0.0 copy-start.1
  192.7 7.5 %fusion = bf16[1,2048,768]{2,1,0:T(8,128)(2,1)} fusion(bf16[1024,768]{1,0:T(8,128)(2,1)S(1)} %copy-done.2, bf16[128,8,2048]{2,1,0:T(8,128)(2,1)} %all-to-all-done), kind=kOutput, calls=%fused_computation.3 | convolution fusion | flops 3222798336 | bytes 8912896 | tf_op jit(solution)/shard_map/dot_general | solution.py:23
  200.2 0.0 copy-done.1
  200.2 0.0 copy-start
  200.2 7.5 %fusion.1 = bf16[1,2048,768]{2,1,0:T(8,128)(2,1)} fusion(bf16[1024,768]{1,0:T(8,128)(2,1)S(1)} %copy-done.1, bf16[128,8,2048]{2,1,0:T(8,128)(2,1)} %all-to-all-done), kind=kOutput, calls=%fused_computation.4 | convolution fusion | flops 3222798336 | bytes 8912896 | tf_op jit(solution)/shard_map/dot_general | solution.py:23
  207.7 0.0 copy-done
  207.7 7.0 %fusion.2 = bf16[1,768,2048]{2,1,0:T(8,128)(2,1)} fusion(bf16[1024,768]{1,0:T(8,128)(2,1)S(1)} %copy-done, bf16[128,8,2048]{2,1,0:T(8,128)(2,1)} %all-to-all-done.2), kind=kOutput, calls=%fused_computation.5 | convolution fusion | flops 3222798336 | bytes 8912896 | tf_op jit(solution)/shard_map/dot_general | solution.py:23
  214.7 6.2 %unpack_mixed.1 = (bf16[128,2048]{1,0:T(8,128)(2,1)}, f32[4,128]{1,0:T(4,128)}) custom-call(s32[4,128]{1,0:T(4,128)} %get-tuple-element.17.slots_ref, f32[4,128]{1,0:T(4,128)} %bitcast.36, bf16[128,2048]{1,0:T(8,128)(2,1)} %cot_ref.3, bf16[1024,2048]{1,0:T(8,128)(2,1)} %bitcast.9.out_ref), custom_call_target="tpu_custom_call" | custom-call | flops 1610612736 | bytes 4194304 | tf_op jit(solution)/shard_map/unpack_mixed/pallas_call | solution.py:245
  220.9 24.3 %all-to-all-done.3 = bf16[128,8,2048]{2,1,0:T(8,128)(2,1)} async-done(((bf16[128,8,2048]{2,1,0:T(8,128)(2,1)}), bf16[128,8,2048]{2,1,0:T(8,128)(2,1)}, u32[]{:S(2)}, u32[]{:S(2)}) %all-to-all-start.3) | async-done | bytes 4194336 | tf_op jit(solution)/shard_map/all_to_all | solution.py:318
  245.2 3.9 %unpack_tokens.1 = bf16[128,2048]{1,0:T(8,128)(2,1)} custom-call(s32[4,128]{1,0:T(4,128)} %get-tuple-element.17.slots_ref, bf16[1024,2048]{1,0:T(8,128)(2,1)} %bitcast.13.din_ref), custom_call_target="tpu_custom_call" | custom-call | flops 536870912 | bytes 4194304 | tf_op jit(solution)/shard_map/unpack_tokens/pallas_call | solution.py:299
Async XLA Ops:
  4.9 64.5 %all-to-all-start = ((bf16[128,8,2048]{2,1,0:T(8,128)(2,1)}), bf16[128,8,2048]{2,1,0:T(8,128)(2,1)}, u32[]{:S(2)}, u32[]{:S(2)}) async-start(bf16[128,8,2048]{2,1,0:T(8,128)(2,1)} %bitcast.33), calls=%async_computation | async-start | bytes 8388608 | tf_op jit(solution)/shard_map/all_to_all | solution.py:318
  69.4 58.6 %all-to-all-start.2 = ((bf16[128,8,2048]{2,1,0:T(8,128)(2,1)}), bf16[128,8,2048]{2,1,0:T(8,128)(2,1)}, u32[]{:S(2)}, u32[]{:S(2)}) async-start(bf16[128,8,2048]{2,1,0:T(8,128)(2,1)} %bitcast.30), calls=%async_computation.2 | async-start | bytes 8388608 | tf_op jit(solution)/shard_map/all_to_all | solution.py:318
  128.0 58.6 %all-to-all-start.1 = ((bf16[128,8,2048]{2,1,0:T(8,128)(2,1)}), bf16[128,8,2048]{2,1,0:T(8,128)(2,1)}, u32[]{:S(2)}, u32[]{:S(2)}) async-start(bf16[128,8,2048]{2,1,0:T(8,128)(2,1)} %bitcast.32), calls=%async_computation.1 | async-start | bytes 8388608 | tf_op jit(solution)/shard_map/all_to_all | solution.py:318
  186.6 6.1 %copy-start.2 = (bf16[1024,768]{1,0:T(8,128)(2,1)S(1)}, bf16[1024,768]{1,0:T(8,128)(2,1)}, u32[]{:S(2)}) copy-start(bf16[1024,768]{1,0:T(8,128)(2,1)} %get-tuple-element.25) | copy-start | bytes 4718596
  186.6 58.6 %all-to-all-start.3 = ((bf16[128,8,2048]{2,1,0:T(8,128)(2,1)}), bf16[128,8,2048]{2,1,0:T(8,128)(2,1)}, u32[]{:S(2)}, u32[]{:S(2)}) async-start(bf16[128,8,2048]{2,1,0:T(8,128)(2,1)} %bitcast.31), calls=%async_computation.3 | async-start | bytes 8388608 | tf_op jit(solution)/shard_map/all_to_all | solution.py:318
  192.7 7.5 %copy-start.1 = (bf16[1024,768]{1,0:T(8,128)(2,1)S(1)}, bf16[1024,768]{1,0:T(8,128)(2,1)}, u32[]{:S(2)}) copy-start(bf16[1024,768]{1,0:T(8,128)(2,1)} %get-tuple-element.26) | copy-start | bytes 4718596
  200.2 7.5 %copy-start = (bf16[1024,768]{1,0:T(8,128)(2,1)S(1)}, bf16[1024,768]{1,0:T(8,128)(2,1)}, u32[]{:S(2)}) copy-start(bf16[1024,768]{1,0:T(8,128)(2,1)} %get-tuple-element.27) | copy-start | bytes 4718596

commit v4 on v3

--- a/solution.py
+++ b/solution.py
@@ -1,6 +1,8 @@
 import functools
+import math
 import jax
 import jax.numpy as jnp
+import numpy as np
 from jax import lax
 from jax.experimental import pallas as pl
 from jax.experimental.pallas import tpu as pltpu
@@ -21,6 +23,31 @@
 
 def dot(a, b, dims=(((1,), (0,)), ((), ()))):
     return lax.dot_general(a, b, dims, preferred_element_type=F32)
+
+
+def send_order(columns_, rows_):
+    side = math.isqrt(columns_)
+    cores = 2 if rows_ % 2 == 0 else 1
+    lines = rows_ // cores
+    x = (columns_ // side, side * rows_)
+    z = (side, rows_)
+    y = (lines, cores)
+    core = (cores, 1)
+    return (z, core, x, y)
+
+
+def block_of(number, order):
+    block = jnp.zeros_like(number)
+    for size, stride in order:
+        block = block * size + (number // stride) % size
+    return block
+
+
+def devices_of(order):
+    devices = np.zeros((1,), np.int64)
+    for size, stride in order:
+        devices = (devices[:, None] + np.arange(size) * stride).reshape(-1)
+    return [int(device) for device in devices]
 
 
 def route_slots(ids, placement, cap):
@@ -58,9 +85,9 @@
     return hits, chosen.astype(F32).astype(BF16), high, low
 
 
-def slots_kernel(cap, chunks, ids_ref, placement_ref, tokens_ref, out_ref, slots_ref, rows_ref, sems):
+def slots_kernel(cap, chunks, order, ids_ref, placement_ref, tokens_ref, out_ref, slots_ref, rows_ref, sems):
     size = rows_ref.shape[1]
-    slots = route_slots(ids_ref[...], placement_ref[...], cap)
+    slots = route_slots(ids_ref[...], block_of(placement_ref[...], order), cap)
     slots_ref[...] = slots
     copies = []
     for i in range(chunks):
@@ -101,14 +128,14 @@
     return pl.CostEstimate(flops=flops, bytes_accessed=moved, transcendentals=0)
 
 
-def pack_tokens(ids, placement, tokens, cap, chunks=PACK_CHUNKS):
+def pack_tokens(ids, placement, tokens, cap, order, chunks=PACK_CHUNKS):
     top, tok_dev = ids.shape
     experts = placement.shape[1]
     width = tokens.shape[1]
     total = experts * cap
     in_vmem = pl.BlockSpec(memory_space=pltpu.VMEM)
     return pl.pallas_call(
-        functools.partial(slots_kernel, cap, chunks),
+        functools.partial(slots_kernel, cap, chunks, order),
         in_specs=[in_vmem] * 3,
         out_specs=[pl.BlockSpec(memory_space=pl.ANY), in_vmem],
         out_shape=[
@@ -313,7 +340,7 @@
     )(slots, d_inputs)
 
 
-def exchange(buffer, experts):
+def exchange(buffer, experts, order):
     total, width = buffer.shape
     moved = lax.all_to_all(
         buffer.reshape(experts, total // experts, width),
@@ -321,11 +348,12 @@
         split_axis=0,
         concat_axis=0,
         tiled=True,
+        axis_index_groups=[devices_of(order)],
     )
     return moved.reshape(total, width)
 
 
-def per_device(tokens, route_weight, expert_ids, placement, w_gate, w_up, w_down, cotangent):
+def per_device(order, tokens, route_weight, expert_ids, placement, w_gate, w_up, w_down, cotangent):
     tok_dev, width = tokens.shape
     fan_out = expert_ids.shape[1]
     experts = placement.shape[0]
@@ -333,14 +361,14 @@
     weights = route_weight.T
     gate, up, down = w_gate[0], w_up[0], w_down[0]
     packed, slots = pack_tokens(
-        expert_ids.T, placement.reshape(1, experts), tokens, cap
-    )
-    inputs = exchange(packed, experts)
-    scaled = exchange(pack_scaled(slots, weights, cotangent, experts * cap), experts)
+        expert_ids.T, placement.reshape(1, experts), tokens, cap, order
+    )
+    inputs = exchange(packed, experts, order)
+    scaled = exchange(pack_scaled(slots, weights, cotangent, experts * cap), experts, order)
     outcome, gate_pre, up_proj, hidden = forward(inputs, gate, up, down)
-    outcome = exchange(outcome, experts)
+    outcome = exchange(outcome, experts, order)
     d_inputs, d_gate, d_up = backward(scaled, gate_pre, up_proj, gate, up, down)
-    returned = exchange(d_inputs, experts)
+    returned = exchange(d_inputs, experts, order)
     grad_gate = dot(inputs, d_gate, FIRST_FIRST).astype(BF16)
     grad_up = dot(inputs, d_up, FIRST_FIRST).astype(BF16)
     grad_down = dot(hidden, scaled, FIRST_FIRST).astype(BF16)
@@ -352,8 +380,9 @@
 def solution(mesh):
     split = P(("col", "row"), None)
     split3 = P(("col", "row"), None, None)
+    order = send_order(mesh.shape["col"], mesh.shape["row"])
     return jax.shard_map(
-        per_device,
+        functools.partial(per_device, order),
         mesh=mesh,
         in_specs=(split, split, split, P(), split3, split3, split3, split),
         out_specs=(split, split, split, split3, split3, split3),

time: 250 us -> 245 us (0.980)
  starting transfers between devices: 30.1 us -> 26.6 us
    all_to_all x4, starting transfers between devices: 30.1 us -> 26.6 us  [exchange(): lax.all_to_all(buffer.reshape(experts, total // experts, width), ('col',...]
where the time goes in v4:
time: 245 us
  waiting for transfers between devices  140 us (57%)
  Pallas kernels  55 us (22%)
  starting transfers between devices  26.6 us (11%)
  matrix products  22 us (9%)
    all_to_all x4, waiting for transfers between devices, exchange(): lax.all_to_all(buffer.reshape(experts, total // experts, width), ('col',...  140 us
    all_to_all x4, starting transfers between devices, exchange(): lax.all_to_all(buffer.reshape(experts, total // experts, width), ('col',...  26.6 us
    dot_general x3, matrix products, dot(): return lax.dot_general(a, b, dims, preferred_element_type=F32)  22 us
    pallas_call x1, Pallas kernels, backward(): pl.pallas_call(backward_kernel, grid=(total // block,), in_specs=[strip(b...  19.7 us
    pallas_call x1, Pallas kernels, forward(): pl.pallas_call(forward_kernel, grid=(total // block,), in_specs=[strip(bl...  15.6 us
    pallas_call x1, Pallas kernels, unpack_mixed(): pl.pallas_call(mixed_kernel, grid=(width // block,), in_specs=[whole((top...  6.21 us
    pallas_call x1, Pallas kernels, pack_scaled(): pl.pallas_call(scaled_kernel, grid=(total // block,), in_specs=[whole((to...  5.28 us
  transfers between devices with their start and end apart: 4, of which 4 were waited for; matrix products, arithmetic and copies ran while one was open for 9% of the time, Pallas kernels for 19%

profile of v4, /device:TPU:1, one launch (start us, length us, event | category | flops | bytes accessed | tf_op | source)
XLA Modules:
  0.0 244.5 jit_solution(1106684381200810395)
XLA Ops:
  0.6 4.3 %pack_tokens.1 = (bf16[1024,2048]{1,0:T(8,128)(2,1)}, s32[4,128]{1,0:T(4,128)}) custom-call(s32[4,128]{1,0:T(4,128)} %bitcast.34, s32[1,128]{1,0:T(1,128)} %bitcast.37, bf16[128,2048]{1,0:T(8,128)(2,1)} %tokens_ref.1), custom_call_target="tpu_custom_call" | custom-call | tf_op jit(solution)/shard_map/pack_tokens/pallas_call | solution.py:137
  4.9 12.0 %all-to-all-start = ((bf16[128,8,2048]{2,1,0:T(8,128)(2,1)}), bf16[128,8,2048]{2,1,0:T(8,128)(2,1)}, u32[]{:S(2)}, u32[]{:S(2)}) async-start(bf16[128,8,2048]{2,1,0:T(8,128)(2,1)} %bitcast.33), calls=%async_computation | async-start | bytes 8388608 | tf_op jit(solution)/shard_map/all_to_all | solution.py:345
  16.9 5.3 %pack_scaled.1 = bf16[1024,2048]{1,0:T(8,128)(2,1)} custom-call(s32[4,128]{1,0:T(4,128)} %get-tuple-element.17.slots_ref, f32[4,128]{1,0:T(4,128)} %bitcast.35, bf16[128,2048]{1,0:T(8,128)(2,1)} %cot_ref.3), custom_call_target="tpu_custom_call" | custom-call | flops 1073741824 | bytes 4194304 | tf_op jit(solution)/shard_map/pack_scaled/pallas_call | solution.py:158
  22.2 47.0 %all-to-all-done = bf16[128,8,2048]{2,1,0:T(8,128)(2,1)} async-done(((bf16[128,8,2048]{2,1,0:T(8,128)(2,1)}), bf16[128,8,2048]{2,1,0:T(8,128)(2,1)}, u32[]{:S(2)}, u32[]{:S(2)}) %all-to-all-start) | async-done | bytes 4194336 | tf_op jit(solution)/shard_map/all_to_all | solution.py:345
  69.2 4.8 %all-to-all-start.2 = ((bf16[128,8,2048]{2,1,0:T(8,128)(2,1)}), bf16[128,8,2048]{2,1,0:T(8,128)(2,1)}, u32[]{:S(2)}, u32[]{:S(2)}) async-start(bf16[128,8,2048]{2,1,0:T(8,128)(2,1)} %bitcast.30), calls=%async_computation.2 | async-start | bytes 8388608 | tf_op jit(solution)/shard_map/all_to_all | solution.py:345
  74.0 15.6 %expert_forward.1 = (bf16[1024,2048]{1,0:T(8,128)(2,1)}, f32[1024,768]{1,0:T(8,128)}, f32[1024,768]{1,0:T(8,128)}, bf16[1024,768]{1,0:T(8,128)(2,1)}) custom-call(bf16[1024,2048]{1,0:T(8,128)(2,1)} %bitcast.4.rows_ref, bf16[2048,768]{1,0:T(8,128)(2,1)} %bitcast.38, bf16[2048,768]{1,0:T(8,128)(2,1)} %bitcast.40, bf16[768,2048]{1,0:T(8,128)(2,1)} %bitcast.42), custom_call_target="tpu_custom_call" | custom-call | flops 9663676416 | bytes 25690112 | tf_op jit(solution)/shard_map/expert_forward/pallas_call | solution.py:185
  89.6 36.6 %all-to-all-done.2 = bf16[128,8,2048]{2,1,0:T(8,128)(2,1)} async-done(((bf16[128,8,2048]{2,1,0:T(8,128)(2,1)}), bf16[128,8,2048]{2,1,0:T(8,128)(2,1)}, u32[]{:S(2)}, u32[]{:S(2)}) %all-to-all-start.2) | async-done | bytes 4194336 | tf_op jit(solution)/shard_map/all_to_all | solution.py:345
  126.2 4.8 %all-to-all-start.1 = ((bf16[128,8,2048]{2,1,0:T(8,128)(2,1)}), bf16[128,8,2048]{2,1,0:T(8,128)(2,1)}, u32[]{:S(2)}, u32[]{:S(2)}) async-start(bf16[128,8,2048]{2,1,0:T(8,128)(2,1)} %bitcast.32), calls=%async_computation.1 | async-start | bytes 8388608 | tf_op jit(solution)/shard_map/all_to_all | solution.py:345
  131.0 19.7 %expert_backward.1 = (bf16[1024,2048]{1,0:T(8,128)(2,1)}, bf16[1024,768]{1,0:T(8,128)(2,1)}, bf16[1024,768]{1,0:T(8,128)(2,1)}) custom-call(bf16[1024,2048]{1,0:T(8,128)(2,1)} %bitcast.11.rows_ref, f32[1024,768]{1,0:T(8,128)} %get-tuple-element.21.gate_pre_ref, f32[1024,768]{1,0:T(8,128)} %get-tuple-element.22.up_proj_ref, bf16[2048,768]{1,0:T(8,128)(2,1)} %bitcast.39, ...), custom_call_target="tpu_custom_call" | custom-call | flops 9663676416 | bytes 27262976 | tf_op jit(solution)/shard_map/expert_backward/pallas_call | solution.py:219
  150.8 32.5 %all-to-all-done.1 = bf16[128,8,2048]{2,1,0:T(8,128)(2,1)} async-done(((bf16[128,8,2048]{2,1,0:T(8,128)(2,1)}), bf16[128,8,2048]{2,1,0:T(8,128)(2,1)}, u32[]{:S(2)}, u32[]{:S(2)}) %all-to-all-start.1) | async-done | bytes 4194336 | tf_op jit(solution)/shard_map/all_to_all | solution.py:345
  183.3 0.0 copy-start.2
  183.3 5.1 %all-to-all-start.3 = ((bf16[128,8,2048]{2,1,0:T(8,128)(2,1)}), bf16[128,8,2048]{2,1,0:T(8,128)(2,1)}, u32[]{:S(2)}, u32[]{:S(2)}) async-start(bf16[128,8,2048]{2,1,0:T(8,128)(2,1)} %bitcast.31), calls=%async_computation.3 | async-start | bytes 8388608 | tf_op jit(solution)/shard_map/all_to_all | solution.py:345
  188.4 0.0 copy-done.2
  188.4 0.0 copy-start.1
  188.4 7.5 %fusion = bf16[1,2048,768]{2,1,0:T(8,128)(2,1)} fusion(bf16[1024,768]{1,0:T(8,128)(2,1)S(1)} %copy-done.2, bf16[128,8,2048]{2,1,0:T(8,128)(2,1)} %all-to-all-done), kind=kOutput, calls=%fused_computation.3 | convolution fusion | flops 3222798336 | bytes 8912896 | tf_op jit(solution)/shard_map/dot_general | solution.py:25
  195.9 0.0 copy-done.1
  195.9 0.0 copy-start
  195.9 7.5 %fusion.1 = bf16[1,2048,768]{2,1,0:T(8,128)(2,1)} fusion(bf16[1024,768]{1,0:T(8,128)(2,1)S(1)} %copy-done.1, bf16[128,8,2048]{2,1,0:T(8,128)(2,1)} %all-to-all-done), kind=kOutput, calls=%fused_computation.4 | convolution fusion | flops 3222798336 | bytes 8912896 | tf_op jit(solution)/shard_map/dot_general | solution.py:25
  203.4 0.0 copy-done
  203.4 7.0 %fusion.2 = bf16[1,768,2048]{2,1,0:T(8,128)(2,1)} fusion(bf16[1024,768]{1,0:T(8,128)(2,1)S(1)} %copy-done, bf16[128,8,2048]{2,1,0:T(8,128)(2,1)} %all-to-all-done.2), kind=kOutput, calls=%fused_computation.5 | convolution fusion | flops 3222798336 | bytes 8912896 | tf_op jit(solution)/shard_map/dot_general | solution.py:25
  210.4 6.2 %unpack_mixed.1 = (bf16[128,2048]{1,0:T(8,128)(2,1)}, f32[4,128]{1,0:T(4,128)}) custom-call(s32[4,128]{1,0:T(4,128)} %get-tuple-element.17.slots_ref, f32[4,128]{1,0:T(4,128)} %bitcast.36, bf16[128,2048]{1,0:T(8,128)(2,1)} %cot_ref.3, bf16[1024,2048]{1,0:T(8,128)(2,1)} %bitcast.9.out_ref), custom_call_target="tpu_custom_call" | custom-call | flops 1610612736 | bytes 4194304 | tf_op jit(solution)/shard_map/unpack_mixed/pallas_call | solution.py:272
  216.6 23.8 %all-to-all-done.3 = bf16[128,8,2048]{2,1,0:T(8,128)(2,1)} async-done(((bf16[128,8,2048]{2,1,0:T(8,128)(2,1)}), bf16[128,8,2048]{2,1,0:T(8,128)(2,1)}, u32[]{:S(2)}, u32[]{:S(2)}) %all-to-all-start.3) | async-done | bytes 4194336 | tf_op jit(solution)/shard_map/all_to_all | solution.py:345
  240.4 3.9 %unpack_tokens.1 = bf16[128,2048]{1,0:T(8,128)(2,1)} custom-call(s32[4,128]{1,0:T(4,128)} %get-tuple-element.17.slots_ref, bf16[1024,2048]{1,0:T(8,128)(2,1)} %bitcast.13.din_ref), custom_call_target="tpu_custom_call" | custom-call | flops 536870912 | bytes 4194304 | tf_op jit(solution)/shard_map/unpack_tokens/pallas_call | solution.py:326
Async XLA Ops:
  4.9 64.3 %all-to-all-start = ((bf16[128,8,2048]{2,1,0:T(8,128)(2,1)}), bf16[128,8,2048]{2,1,0:T(8,128)(2,1)}, u32[]{:S(2)}, u32[]{:S(2)}) async-start(bf16[128,8,2048]{2,1,0:T(8,128)(2,1)} %bitcast.33), calls=%async_computation | async-start | bytes 8388608 | tf_op jit(solution)/shard_map/all_to_all | solution.py:345
  69.2 57.0 %all-to-all-start.2 = ((bf16[128,8,2048]{2,1,0:T(8,128)(2,1)}), bf16[128,8,2048]{2,1,0:T(8,128)(2,1)}, u32[]{:S(2)}, u32[]{:S(2)}) async-start(bf16[128,8,2048]{2,1,0:T(8,128)(2,1)} %bitcast.30), calls=%async_computation.2 | async-start | bytes 8388608 | tf_op jit(solution)/shard_map/all_to_all | solution.py:345
  126.2 57.0 %all-to-all-start.1 = ((bf16[128,8,2048]{2,1,0:T(8,128)(2,1)}), bf16[128,8,2048]{2,1,0:T(8,128)(2,1)}, u32[]{:S(2)}, u32[]{:S(2)}) async-start(bf16[128,8,2048]{2,1,0:T(8,128)(2,1)} %bitcast.32), calls=%async_computation.1 | async-start | bytes 8388608 | tf_op jit(solution)/shard_map/all_to_all | solution.py:345
  183.3 5.1 %copy-start.2 = (bf16[1024,768]{1,0:T(8,128)(2,1)S(1)}, bf16[1024,768]{1,0:T(8,128)(2,1)}, u32[]{:S(2)}) copy-start(bf16[1024,768]{1,0:T(8,128)(2,1)} %get-tuple-element.25) | copy-start | bytes 4718596
  183.3 57.2 %all-to-all-start.3 = ((bf16[128,8,2048]{2,1,0:T(8,128)(2,1)}), bf16[128,8,2048]{2,1,0:T(8,128)(2,1)}, u32[]{:S(2)}, u32[]{:S(2)}) async-start(bf16[128,8,2048]{2,1,0:T(8,128)(2,1)} %bitcast.31), calls=%async_computation.3 | async-start | bytes 8388608 | tf_op jit(solution)/shard_map/all_to_all | solution.py:345
  188.4 7.5 %copy-start.1 = (bf16[1024,768]{1,0:T(8,128)(2,1)S(1)}, bf16[1024,768]{1,0:T(8,128)(2,1)}, u32[]{:S(2)}) copy-start(bf16[1024,768]{1,0:T(8,128)(2,1)} %get-tuple-element.26) | copy-start | bytes 4718596
  195.9 7.5 %copy-start = (bf16[1024,768]{1,0:T(8,128)(2,1)S(1)}, bf16[1024,768]{1,0:T(8,128)(2,1)}, u32[]{:S(2)}) copy-start(bf16[1024,768]{1,0:T(8,128)(2,1)} %get-tuple-element.27) | copy-start | bytes 4718596

commit v5 on v4

--- a/solution.py
+++ b/solution.py
@@ -29,24 +29,29 @@
     side = math.isqrt(columns_)
     cores = 2 if rows_ % 2 == 0 else 1
     lines = rows_ // cores
-    x = (columns_ // side, side * rows_)
-    z = (side, rows_)
-    y = (lines, cores)
-    core = (cores, 1)
+    x = (columns_ // side, side * rows_, False)
+    z = (side, rows_, side == 4)
+    y = (lines, cores, False)
+    core = (cores, 1, False)
     return (z, core, x, y)
+
+
+def digit_of(value, reflected):
+    return value ^ (value >> 1) if reflected else value
 
 
 def block_of(number, order):
     block = jnp.zeros_like(number)
-    for size, stride in order:
-        block = block * size + (number // stride) % size
+    for size, stride, reflected in order:
+        block = block * size + digit_of((number // stride) % size, reflected)
     return block
 
 
 def devices_of(order):
     devices = np.zeros((1,), np.int64)
-    for size, stride in order:
-        devices = (devices[:, None] + np.arange(size) * stride).reshape(-1)
+    for size, stride, reflected in order:
+        steps = digit_of(np.arange(size), reflected) * stride
+        devices = (devices[:, None] + steps).reshape(-1)
     return [int(device) for device in devices]
 
 

time: 245 us -> 248 us (1.012)
  starting transfers between devices: 26.6 us -> 29.1 us
    all_to_all x4, starting transfers between devices: 26.6 us -> 29.1 us  [exchange(): lax.all_to_all(buffer.reshape(experts, total // experts, width), ('col',...]
where the time goes in v5:
time: 248 us
  waiting for transfers between devices  140 us (56%)
  Pallas kernels  55 us (22%)
  starting transfers between devices  29.1 us (12%)
  matrix products  22 us (9%)
    all_to_all x4, waiting for transfers between devices, exchange(): lax.all_to_all(buffer.reshape(experts, total // experts, width), ('col',...  140 us
    all_to_all x4, starting transfers between devices, exchange(): lax.all_to_all(buffer.reshape(experts, total // experts, width), ('col',...  29.1 us
    dot_general x3, matrix products, dot(): return lax.dot_general(a, b, dims, preferred_element_type=F32)  22 us
    pallas_call x1, Pallas kernels, backward(): pl.pallas_call(backward_kernel, grid=(total // block,), in_specs=[strip(b...  19.8 us
    pallas_call x1, Pallas kernels, forward(): pl.pallas_call(forward_kernel, grid=(total // block,), in_specs=[strip(bl...  15.6 us
    pallas_call x1, Pallas kernels, unpack_mixed(): pl.pallas_call(mixed_kernel, grid=(width // block,), in_specs=[whole((top...  6.21 us
    pallas_call x1, Pallas kernels, pack_scaled(): pl.pallas_call(scaled_kernel, grid=(total // block,), in_specs=[whole((to...  5.28 us
  transfers between devices with their start and end apart: 4, of which 4 were waited for; matrix products, arithmetic and copies ran while one was open for 9% of the time, Pallas kernels for 19%

profile of v5, /device:TPU:1, one launch (start us, length us, event | category | flops | bytes accessed | tf_op | source)
XLA Modules:
  0.0 247.5 jit_solution(4152570999966512652)
XLA Ops:
  0.6 4.3 %pack_tokens.1 = (bf16[1024,2048]{1,0:T(8,128)(2,1)}, s32[4,128]{1,0:T(4,128)}) custom-call(s32[4,128]{1,0:T(4,128)} %bitcast.34, s32[1,128]{1,0:T(1,128)} %bitcast.37, bf16[128,2048]{1,0:T(8,128)(2,1)} %tokens_ref.1), custom_call_target="tpu_custom_call" | custom-call | tf_op jit(solution)/shard_map/pack_tokens/pallas_call | solution.py:142
  4.9 12.0 %all-to-all-start = ((bf16[128,8,2048]{2,1,0:T(8,128)(2,1)}), bf16[128,8,2048]{2,1,0:T(8,128)(2,1)}, u32[]{:S(2)}, u32[]{:S(2)}) async-start(bf16[128,8,2048]{2,1,0:T(8,128)(2,1)} %bitcast.33), calls=%async_computation | async-start | bytes 8388608 | tf_op jit(solution)/shard_map/all_to_all | solution.py:350
  16.9 5.3 %pack_scaled.1 = bf16[1024,2048]{1,0:T(8,128)(2,1)} custom-call(s32[4,128]{1,0:T(4,128)} %get-tuple-element.17.slots_ref, f32[4,128]{1,0:T(4,128)} %bitcast.35, bf16[128,2048]{1,0:T(8,128)(2,1)} %cot_ref.3), custom_call_target="tpu_custom_call" | custom-call | flops 1073741824 | bytes 4194304 | tf_op jit(solution)/shard_map/pack_scaled/pallas_call | solution.py:163
  22.2 47.1 %all-to-all-done = bf16[128,8,2048]{2,1,0:T(8,128)(2,1)} async-done(((bf16[128,8,2048]{2,1,0:T(8,128)(2,1)}), bf16[128,8,2048]{2,1,0:T(8,128)(2,1)}, u32[]{:S(2)}, u32[]{:S(2)}) %all-to-all-start) | async-done | bytes 4194336 | tf_op jit(solution)/shard_map/all_to_all | solution.py:350
  69.2 5.7 %all-to-all-start.2 = ((bf16[128,8,2048]{2,1,0:T(8,128)(2,1)}), bf16[128,8,2048]{2,1,0:T(8,128)(2,1)}, u32[]{:S(2)}, u32[]{:S(2)}) async-start(bf16[128,8,2048]{2,1,0:T(8,128)(2,1)} %bitcast.30), calls=%async_computation.2 | async-start | bytes 8388608 | tf_op jit(solution)/shard_map/all_to_all | solution.py:350
  75.0 15.6 %expert_forward.1 = (bf16[1024,2048]{1,0:T(8,128)(2,1)}, f32[1024,768]{1,0:T(8,128)}, f32[1024,768]{1,0:T(8,128)}, bf16[1024,768]{1,0:T(8,128)(2,1)}) custom-call(bf16[1024,2048]{1,0:T(8,128)(2,1)} %bitcast.4.rows_ref, bf16[2048,768]{1,0:T(8,128)(2,1)} %bitcast.38, bf16[2048,768]{1,0:T(8,128)(2,1)} %bitcast.40, bf16[768,2048]{1,0:T(8,128)(2,1)} %bitcast.42), custom_call_target="tpu_custom_call" | custom-call | flops 9663676416 | bytes 25690112 | tf_op jit(solution)/shard_map/expert_forward/pallas_call | solution.py:190
  90.6 36.7 %all-to-all-done.2 = bf16[128,8,2048]{2,1,0:T(8,128)(2,1)} async-done(((bf16[128,8,2048]{2,1,0:T(8,128)(2,1)}), bf16[128,8,2048]{2,1,0:T(8,128)(2,1)}, u32[]{:S(2)}, u32[]{:S(2)}) %all-to-all-start.2) | async-done | bytes 4194336 | tf_op jit(solution)/shard_map/all_to_all | solution.py:350
  127.3 5.7 %all-to-all-start.1 = ((bf16[128,8,2048]{2,1,0:T(8,128)(2,1)}), bf16[128,8,2048]{2,1,0:T(8,128)(2,1)}, u32[]{:S(2)}, u32[]{:S(2)}) async-start(bf16[128,8,2048]{2,1,0:T(8,128)(2,1)} %bitcast.32), calls=%async_computation.1 | async-start | bytes 8388608 | tf_op jit(solution)/shard_map/all_to_all | solution.py:350
  133.0 19.8 %expert_backward.1 = (bf16[1024,2048]{1,0:T(8,128)(2,1)}, bf16[1024,768]{1,0:T(8,128)(2,1)}, bf16[1024,768]{1,0:T(8,128)(2,1)}) custom-call(bf16[1024,2048]{1,0:T(8,128)(2,1)} %bitcast.11.rows_ref, f32[1024,768]{1,0:T(8,128)} %get-tuple-element.21.gate_pre_ref, f32[1024,768]{1,0:T(8,128)} %get-tuple-element.22.up_proj_ref, bf16[2048,768]{1,0:T(8,128)(2,1)} %bitcast.39, ...), custom_call_target="tpu_custom_call" | custom-call | flops 9663676416 | bytes 27262976 | tf_op jit(solution)/shard_map/expert_backward/pallas_call | solution.py:224
  152.8 32.6 %all-to-all-done.1 = bf16[128,8,2048]{2,1,0:T(8,128)(2,1)} async-done(((bf16[128,8,2048]{2,1,0:T(8,128)(2,1)}), bf16[128,8,2048]{2,1,0:T(8,128)(2,1)}, u32[]{:S(2)}, u32[]{:S(2)}) %all-to-all-start.1) | async-done | bytes 4194336 | tf_op jit(solution)/shard_map/all_to_all | solution.py:350
  185.4 0.0 copy-start.2
  185.4 5.7 %all-to-all-start.3 = ((bf16[128,8,2048]{2,1,0:T(8,128)(2,1)}), bf16[128,8,2048]{2,1,0:T(8,128)(2,1)}, u32[]{:S(2)}, u32[]{:S(2)}) async-start(bf16[128,8,2048]{2,1,0:T(8,128)(2,1)} %bitcast.31), calls=%async_computation.3 | async-start | bytes 8388608 | tf_op jit(solution)/shard_map/all_to_all | solution.py:350
  191.1 0.0 copy-done.2
  191.1 0.0 copy-start.1
  191.1 7.5 %fusion = bf16[1,2048,768]{2,1,0:T(8,128)(2,1)} fusion(bf16[1024,768]{1,0:T(8,128)(2,1)S(1)} %copy-done.2, bf16[128,8,2048]{2,1,0:T(8,128)(2,1)} %all-to-all-done), kind=kOutput, calls=%fused_computation.3 | convolution fusion | flops 3222798336 | bytes 8912896 | tf_op jit(solution)/shard_map/dot_general | solution.py:25
  198.6 0.0 copy-done.1
  198.6 0.0 copy-start
  198.6 7.5 %fusion.1 = bf16[1,2048,768]{2,1,0:T(8,128)(2,1)} fusion(bf16[1024,768]{1,0:T(8,128)(2,1)S(1)} %copy-done.1, bf16[128,8,2048]{2,1,0:T(8,128)(2,1)} %all-to-all-done), kind=kOutput, calls=%fused_computation.4 | convolution fusion | flops 3222798336 | bytes 8912896 | tf_op jit(solution)/shard_map/dot_general | solution.py:25
  206.2 0.0 copy-done
  206.2 7.0 %fusion.2 = bf16[1,768,2048]{2,1,0:T(8,128)(2,1)} fusion(bf16[1024,768]{1,0:T(8,128)(2,1)S(1)} %copy-done, bf16[128,8,2048]{2,1,0:T(8,128)(2,1)} %all-to-all-done.2), kind=kOutput, calls=%fused_computation.5 | convolution fusion | flops 3222798336 | bytes 8912896 | tf_op jit(solution)/shard_map/dot_general | solution.py:25
  213.2 6.2 %unpack_mixed.1 = (bf16[128,2048]{1,0:T(8,128)(2,1)}, f32[4,128]{1,0:T(4,128)}) custom-call(s32[4,128]{1,0:T(4,128)} %get-tuple-element.17.slots_ref, f32[4,128]{1,0:T(4,128)} %bitcast.36, bf16[128,2048]{1,0:T(8,128)(2,1)} %cot_ref.3, bf16[1024,2048]{1,0:T(8,128)(2,1)} %bitcast.9.out_ref), custom_call_target="tpu_custom_call" | custom-call | flops 1610612736 | bytes 4194304 | tf_op jit(solution)/shard_map/unpack_mixed/pallas_call | solution.py:277
  219.4 24.1 %all-to-all-done.3 = bf16[128,8,2048]{2,1,0:T(8,128)(2,1)} async-done(((bf16[128,8,2048]{2,1,0:T(8,128)(2,1)}), bf16[128,8,2048]{2,1,0:T(8,128)(2,1)}, u32[]{:S(2)}, u32[]{:S(2)}) %all-to-all-start.3) | async-done | bytes 4194336 | tf_op jit(solution)/shard_map/all_to_all | solution.py:350
  243.5 3.9 %unpack_tokens.1 = bf16[128,2048]{1,0:T(8,128)(2,1)} custom-call(s32[4,128]{1,0:T(4,128)} %get-tuple-element.17.slots_ref, bf16[1024,2048]{1,0:T(8,128)(2,1)} %bitcast.13.din_ref), custom_call_target="tpu_custom_call" | custom-call | flops 536870912 | bytes 4194304 | tf_op jit(solution)/shard_map/unpack_tokens/pallas_call | solution.py:331
Async XLA Ops:
  4.9 64.3 %all-to-all-start = ((bf16[128,8,2048]{2,1,0:T(8,128)(2,1)}), bf16[128,8,2048]{2,1,0:T(8,128)(2,1)}, u32[]{:S(2)}, u32[]{:S(2)}) async-start(bf16[128,8,2048]{2,1,0:T(8,128)(2,1)} %bitcast.33), calls=%async_computation | async-start | bytes 8388608 | tf_op jit(solution)/shard_map/all_to_all | solution.py:350
  69.2 58.1 %all-to-all-start.2 = ((bf16[128,8,2048]{2,1,0:T(8,128)(2,1)}), bf16[128,8,2048]{2,1,0:T(8,128)(2,1)}, u32[]{:S(2)}, u32[]{:S(2)}) async-start(bf16[128,8,2048]{2,1,0:T(8,128)(2,1)} %bitcast.30), calls=%async_computation.2 | async-start | bytes 8388608 | tf_op jit(solution)/shard_map/all_to_all | solution.py:350
  127.3 58.1 %all-to-all-start.1 = ((bf16[128,8,2048]{2,1,0:T(8,128)(2,1)}), bf16[128,8,2048]{2,1,0:T(8,128)(2,1)}, u32[]{:S(2)}, u32[]{:S(2)}) async-start(bf16[128,8,2048]{2,1,0:T(8,128)(2,1)} %bitcast.32), calls=%async_computation.1 | async-start | bytes 8388608 | tf_op jit(solution)/shard_map/all_to_all | solution.py:350
  185.4 5.7 %copy-start.2 = (bf16[1024,768]{1,0:T(8,128)(2,1)S(1)}, bf16[1024,768]{1,0:T(8,128)(2,1)}, u32[]{:S(2)}) copy-start(bf16[1024,768]{1,0:T(8,128)(2,1)} %get-tuple-element.25) | copy-start | bytes 4718596
  185.4 58.1 %all-to-all-start.3 = ((bf16[128,8,2048]{2,1,0:T(8,128)(2,1)}), bf16[128,8,2048]{2,1,0:T(8,128)(2,1)}, u32[]{:S(2)}, u32[]{:S(2)}) async-start(bf16[128,8,2048]{2,1,0:T(8,128)(2,1)} %bitcast.31), calls=%async_computation.3 | async-start | bytes 8388608 | tf_op jit(solution)/shard_map/all_to_all | solution.py:350
  191.1 7.5 %copy-start.1 = (bf16[1024,768]{1,0:T(8,128)(2,1)S(1)}, bf16[1024,768]{1,0:T(8,128)(2,1)}, u32[]{:S(2)}) copy-start(bf16[1024,768]{1,0:T(8,128)(2,1)} %get-tuple-element.26) | copy-start | bytes 4718596
  198.6 7.5 %copy-start = (bf16[1024,768]{1,0:T(8,128)(2,1)S(1)}, bf16[1024,768]{1,0:T(8,128)(2,1)}, u32[]{:S(2)}) copy-start(bf16[1024,768]{1,0:T(8,128)(2,1)} %get-tuple-element.27) | copy-start | bytes 4718596

commit v6 on v4

--- a/solution.py
+++ b/solution.py
@@ -13,7 +13,7 @@
 LAST_LAST = (((1,), (1,)), ((), ()))
 FIRST_FIRST = (((0,), (0,)), ((), ()))
 VMEM_LIMIT = 56 * 1024 * 1024
-PACK_CHUNKS = 4
+PACK_CHUNKS = 8
 UNPACK_CHUNKS = 4
 
 
@@ -33,7 +33,7 @@
     z = (side, rows_)
     y = (lines, cores)
     core = (cores, 1)
-    return (z, core, x, y)
+    return (x, core, z, y)
 
 
 def block_of(number, order):

time: 245 us -> 244 us (level)
  waiting for transfers between devices: 140 us -> 134 us
  starting transfers between devices: 26.6 us -> 31.3 us
    all_to_all x4, waiting for transfers between devices: 140 us -> 134 us  [exchange(): lax.all_to_all(buffer.reshape(experts, total // experts, width), ('col',...]
    all_to_all x4, starting transfers between devices: 26.6 us -> 31.3 us  [exchange(): lax.all_to_all(buffer.reshape(experts, total // experts, width), ('col',...]
where the time goes in v6:
time: 244 us; the launch traced here: 243 us
  waiting for transfers between devices  134 us (55%)
  Pallas kernels  54.9 us (22%)
  starting transfers between devices  31.3 us (13%)
  matrix products  22 us (9%)
    all_to_all x4, waiting for transfers between devices, exchange(): lax.all_to_all(buffer.reshape(experts, total // experts, width), ('col',...  134 us
    all_to_all x4, starting transfers between devices, exchange(): lax.all_to_all(buffer.reshape(experts, total // experts, width), ('col',...  31.3 us
    dot_general x3, matrix products, dot(): return lax.dot_general(a, b, dims, preferred_element_type=F32)  22 us
    pallas_call x1, Pallas kernels, backward(): pl.pallas_call(backward_kernel, grid=(total // block,), in_specs=[strip(b...  19.7 us
    pallas_call x1, Pallas kernels, forward(): pl.pallas_call(forward_kernel, grid=(total // block,), in_specs=[strip(bl...  15.6 us
    pallas_call x1, Pallas kernels, unpack_mixed(): pl.pallas_call(mixed_kernel, grid=(width // block,), in_specs=[whole((top...  6.22 us
    pallas_call x1, Pallas kernels, pack_scaled(): pl.pallas_call(scaled_kernel, grid=(total // block,), in_specs=[whole((to...  5.28 us
  transfers between devices with their start and end apart: 4, of which 4 were waited for; matrix products, arithmetic and copies ran while one was open for 9% of the time, Pallas kernels for 19%

profile of v6, /device:TPU:1, one launch (start us, length us, event | category | flops | bytes accessed | tf_op | source)
XLA Modules:
  0.0 242.9 jit_solution(8855249651327037392)
XLA Ops:
  0.6 4.2 %pack_tokens.1 = (bf16[1024,2048]{1,0:T(8,128)(2,1)}, s32[4,128]{1,0:T(4,128)}) custom-call(s32[4,128]{1,0:T(4,128)} %bitcast.34, s32[1,128]{1,0:T(1,128)} %bitcast.37, bf16[128,2048]{1,0:T(8,128)(2,1)} %tokens_ref.1), custom_call_target="tpu_custom_call" | custom-call | tf_op jit(solution)/shard_map/pack_tokens/pallas_call | solution.py:137
  4.8 12.0 %all-to-all-start = ((bf16[128,8,2048]{2,1,0:T(8,128)(2,1)}), bf16[128,8,2048]{2,1,0:T(8,128)(2,1)}, u32[]{:S(2)}, u32[]{:S(2)}) async-start(bf16[128,8,2048]{2,1,0:T(8,128)(2,1)} %bitcast.33), calls=%async_computation | async-start | bytes 8388608 | tf_op jit(solution)/shard_map/all_to_all | solution.py:345
  16.8 5.3 %pack_scaled.1 = bf16[1024,2048]{1,0:T(8,128)(2,1)} custom-call(s32[4,128]{1,0:T(4,128)} %get-tuple-element.17.slots_ref, f32[4,128]{1,0:T(4,128)} %bitcast.35, bf16[128,2048]{1,0:T(8,128)(2,1)} %cot_ref.3), custom_call_target="tpu_custom_call" | custom-call | flops 1073741824 | bytes 4194304 | tf_op jit(solution)/shard_map/pack_scaled/pallas_call | solution.py:158
  22.1 45.4 %all-to-all-done = bf16[128,8,2048]{2,1,0:T(8,128)(2,1)} async-done(((bf16[128,8,2048]{2,1,0:T(8,128)(2,1)}), bf16[128,8,2048]{2,1,0:T(8,128)(2,1)}, u32[]{:S(2)}, u32[]{:S(2)}) %all-to-all-start) | async-done | bytes 4194336 | tf_op jit(solution)/shard_map/all_to_all | solution.py:345
  67.5 6.4 %all-to-all-start.2 = ((bf16[128,8,2048]{2,1,0:T(8,128)(2,1)}), bf16[128,8,2048]{2,1,0:T(8,128)(2,1)}, u32[]{:S(2)}, u32[]{:S(2)}) async-start(bf16[128,8,2048]{2,1,0:T(8,128)(2,1)} %bitcast.30), calls=%async_computation.2 | async-start | bytes 8388608 | tf_op jit(solution)/shard_map/all_to_all | solution.py:345
  73.9 15.6 %expert_forward.1 = (bf16[1024,2048]{1,0:T(8,128)(2,1)}, f32[1024,768]{1,0:T(8,128)}, f32[1024,768]{1,0:T(8,128)}, bf16[1024,768]{1,0:T(8,128)(2,1)}) custom-call(bf16[1024,2048]{1,0:T(8,128)(2,1)} %bitcast.4.rows_ref, bf16[2048,768]{1,0:T(8,128)(2,1)} %bitcast.38, bf16[2048,768]{1,0:T(8,128)(2,1)} %bitcast.40, bf16[768,2048]{1,0:T(8,128)(2,1)} %bitcast.42), custom_call_target="tpu_custom_call" | custom-call | flops 9663676416 | bytes 25690112 | tf_op jit(solution)/shard_map/expert_forward/pallas_call | solution.py:185
  89.5 35.0 %all-to-all-done.2 = bf16[128,8,2048]{2,1,0:T(8,128)(2,1)} async-done(((bf16[128,8,2048]{2,1,0:T(8,128)(2,1)}), bf16[128,8,2048]{2,1,0:T(8,128)(2,1)}, u32[]{:S(2)}, u32[]{:S(2)}) %all-to-all-start.2) | async-done | bytes 4194336 | tf_op jit(solution)/shard_map/all_to_all | solution.py:345
  124.6 6.4 %all-to-all-start.1 = ((bf16[128,8,2048]{2,1,0:T(8,128)(2,1)}), bf16[128,8,2048]{2,1,0:T(8,128)(2,1)}, u32[]{:S(2)}, u32[]{:S(2)}) async-start(bf16[128,8,2048]{2,1,0:T(8,128)(2,1)} %bitcast.32), calls=%async_computation.1 | async-start | bytes 8388608 | tf_op jit(solution)/shard_map/all_to_all | solution.py:345
  131.0 19.7 %expert_backward.1 = (bf16[1024,2048]{1,0:T(8,128)(2,1)}, bf16[1024,768]{1,0:T(8,128)(2,1)}, bf16[1024,768]{1,0:T(8,128)(2,1)}) custom-call(bf16[1024,2048]{1,0:T(8,128)(2,1)} %bitcast.11.rows_ref, f32[1024,768]{1,0:T(8,128)} %get-tuple-element.21.gate_pre_ref, f32[1024,768]{1,0:T(8,128)} %get-tuple-element.22.up_proj_ref, bf16[2048,768]{1,0:T(8,128)(2,1)} %bitcast.39, ...), custom_call_target="tpu_custom_call" | custom-call | flops 9663676416 | bytes 27262976 | tf_op jit(solution)/shard_map/expert_backward/pallas_call | solution.py:219
  150.8 30.9 %all-to-all-done.1 = bf16[128,8,2048]{2,1,0:T(8,128)(2,1)} async-done(((bf16[128,8,2048]{2,1,0:T(8,128)(2,1)}), bf16[128,8,2048]{2,1,0:T(8,128)(2,1)}, u32[]{:S(2)}, u32[]{:S(2)}) %all-to-all-start.1) | async-done | bytes 4194336 | tf_op jit(solution)/shard_map/all_to_all | solution.py:345
  181.7 0.0 copy-start.2
  181.7 6.4 %all-to-all-start.3 = ((bf16[128,8,2048]{2,1,0:T(8,128)(2,1)}), bf16[128,8,2048]{2,1,0:T(8,128)(2,1)}, u32[]{:S(2)}, u32[]{:S(2)}) async-start(bf16[128,8,2048]{2,1,0:T(8,128)(2,1)} %bitcast.31), calls=%async_computation.3 | async-start | bytes 8388608 | tf_op jit(solution)/shard_map/all_to_all | solution.py:345
  188.1 0.0 copy-done.2
  188.1 0.0 copy-start.1
  188.2 7.5 %fusion = bf16[1,2048,768]{2,1,0:T(8,128)(2,1)} fusion(bf16[1024,768]{1,0:T(8,128)(2,1)S(1)} %copy-done.2, bf16[128,8,2048]{2,1,0:T(8,128)(2,1)} %all-to-all-done), kind=kOutput, calls=%fused_computation.3 | convolution fusion | flops 3222798336 | bytes 8912896 | tf_op jit(solution)/shard_map/dot_general | solution.py:25
  195.7 0.0 copy-done.1
  195.7 0.0 copy-start
  195.7 7.5 %fusion.1 = bf16[1,2048,768]{2,1,0:T(8,128)(2,1)} fusion(bf16[1024,768]{1,0:T(8,128)(2,1)S(1)} %copy-done.1, bf16[128,8,2048]{2,1,0:T(8,128)(2,1)} %all-to-all-done), kind=kOutput, calls=%fused_computation.4 | convolution fusion | flops 3222798336 | bytes 8912896 | tf_op jit(solution)/shard_map/dot_general | solution.py:25
  203.2 0.0 copy-done
  203.2 7.0 %fusion.2 = bf16[1,768,2048]{2,1,0:T(8,128)(2,1)} fusion(bf16[1024,768]{1,0:T(8,128)(2,1)S(1)} %copy-done, bf16[128,8,2048]{2,1,0:T(8,128)(2,1)} %all-to-all-done.2), kind=kOutput, calls=%fused_computation.5 | convolution fusion | flops 3222798336 | bytes 8912896 | tf_op jit(solution)/shard_map/dot_general | solution.py:25
  210.2 6.2 %unpack_mixed.1 = (bf16[128,2048]{1,0:T(8,128)(2,1)}, f32[4,128]{1,0:T(4,128)}) custom-call(s32[4,128]{1,0:T(4,128)} %get-tuple-element.17.slots_ref, f32[4,128]{1,0:T(4,128)} %bitcast.36, bf16[128,2048]{1,0:T(8,128)(2,1)} %cot_ref.3, bf16[1024,2048]{1,0:T(8,128)(2,1)} %bitcast.9.out_ref), custom_call_target="tpu_custom_call" | custom-call | flops 1610612736 | bytes 4194304 | tf_op jit(solution)/shard_map/unpack_mixed/pallas_call | solution.py:272
  216.4 22.4 %all-to-all-done.3 = bf16[128,8,2048]{2,1,0:T(8,128)(2,1)} async-done(((bf16[128,8,2048]{2,1,0:T(8,128)(2,1)}), bf16[128,8,2048]{2,1,0:T(8,128)(2,1)}, u32[]{:S(2)}, u32[]{:S(2)}) %all-to-all-start.3) | async-done | bytes 4194336 | tf_op jit(solution)/shard_map/all_to_all | solution.py:345
  238.8 3.9 %unpack_tokens.1 = bf16[128,2048]{1,0:T(8,128)(2,1)} custom-call(s32[4,128]{1,0:T(4,128)} %get-tuple-element.17.slots_ref, bf16[1024,2048]{1,0:T(8,128)(2,1)} %bitcast.13.din_ref), custom_call_target="tpu_custom_call" | custom-call | flops 536870912 | bytes 4194304 | tf_op jit(solution)/shard_map/unpack_tokens/pallas_call | solution.py:326
Async XLA Ops:
  4.8 62.7 %all-to-all-start = ((bf16[128,8,2048]{2,1,0:T(8,128)(2,1)}), bf16[128,8,2048]{2,1,0:T(8,128)(2,1)}, u32[]{:S(2)}, u32[]{:S(2)}) async-start(bf16[128,8,2048]{2,1,0:T(8,128)(2,1)} %bitcast.33), calls=%async_computation | async-start | bytes 8388608 | tf_op jit(solution)/shard_map/all_to_all | solution.py:345
  67.5 57.1 %all-to-all-start.2 = ((bf16[128,8,2048]{2,1,0:T(8,128)(2,1)}), bf16[128,8,2048]{2,1,0:T(8,128)(2,1)}, u32[]{:S(2)}, u32[]{:S(2)}) async-start(bf16[128,8,2048]{2,1,0:T(8,128)(2,1)} %bitcast.30), calls=%async_computation.2 | async-start | bytes 8388608 | tf_op jit(solution)/shard_map/all_to_all | solution.py:345
  124.6 57.1 %all-to-all-start.1 = ((bf16[128,8,2048]{2,1,0:T(8,128)(2,1)}), bf16[128,8,2048]{2,1,0:T(8,128)(2,1)}, u32[]{:S(2)}, u32[]{:S(2)}) async-start(bf16[128,8,2048]{2,1,0:T(8,128)(2,1)} %bitcast.32), calls=%async_computation.1 | async-start | bytes 8388608 | tf_op jit(solution)/shard_map/all_to_all | solution.py:345
  181.7 6.5 %copy-start.2 = (bf16[1024,768]{1,0:T(8,128)(2,1)S(1)}, bf16[1024,768]{1,0:T(8,128)(2,1)}, u32[]{:S(2)}) copy-start(bf16[1024,768]{1,0:T(8,128)(2,1)} %get-tuple-element.25) | copy-start | bytes 4718596
  181.7 57.1 %all-to-all-start.3 = ((bf16[128,8,2048]{2,1,0:T(8,128)(2,1)}), bf16[128,8,2048]{2,1,0:T(8,128)(2,1)}, u32[]{:S(2)}, u32[]{:S(2)}) async-start(bf16[128,8,2048]{2,1,0:T(8,128)(2,1)} %bitcast.31), calls=%async_computation.3 | async-start | bytes 8388608 | tf_op jit(solution)/shard_map/all_to_all | solution.py:345
  188.1 7.5 %copy-start.1 = (bf16[1024,768]{1,0:T(8,128)(2,1)S(1)}, bf16[1024,768]{1,0:T(8,128)(2,1)}, u32[]{:S(2)}) copy-start(bf16[1024,768]{1,0:T(8,128)(2,1)} %get-tuple-element.26) | copy-start | bytes 4718596
  195.7 7.5 %copy-start = (bf16[1024,768]{1,0:T(8,128)(2,1)S(1)}, bf16[1024,768]{1,0:T(8,128)(2,1)}, u32[]{:S(2)}) copy-start(bf16[1024,768]{1,0:T(8,128)(2,1)} %get-tuple-element.27) | copy-start | bytes 4718596
